TPU v7x, 32 devices: a whole 2x2x4 slice. The times are simulated.
32 devices in a mesh: groups: 2 (over y), ctx: 16 (over z, x, core).
Axes of the slice: x: 2, y: 2, z: 4, core: 2. Of those that a mesh axis runs over, the one named last changes fastest.
Arguments:
- queries: bfloat16 [8192, 8192], P(('groups', 'ctx')), parts along dimension 0, may hold values from -10 to 10
- keys: bfloat16 [8192, 1024], P(('groups', 'ctx')), parts along dimension 0, may hold values from -6 to 6
- values: bfloat16 [8192, 1024], P(('groups', 'ctx')), parts along dimension 0, may hold values from -6 to 6
- positions: int32 [8192], P(('groups', 'ctx')), parts along dimension 0, may hold values from 0 to 4096, as said below
- picks: int32 [64, 8, 2], P(('groups', 'ctx')), parts along dimension 0, may hold values from -1 to 31, as said below
Outputs:
- attended: bfloat16 [8192, 8192], P(('groups', 'ctx')), parts along dimension 0
There are 2 independent parts, one for each index of `groups`. A program takes and returns all parts, laid end to end along the dimension named above; each array names one. Nothing has to cross between parts.
Inputs may be any that keep to these rules, and one draw needn't show every extreme that they name: positions never fall from one token to the next and each lies in [index, index + 1]; the first is 0 and the last is 4096. A pick of query block b is -1 or a block held by an earlier shard, so its index is below (b // 2) * 2; it may lie inside the band, and then its keys count twice; the two picks of one query block and head differ when both are set, and both are set or both -1; over the 2 query blocks of one shard and all heads, at most 2 picks name blocks of one shard, and some shard has exactly 2 for some other shard in every draw.
All inputs are finite; a program needn't handle non-finite values.
Results may differ from a plain program's by a relative error of at most 0.009.
Values may be sent and summed in bfloat16 or wider, within the bound.
A program may use at most 192 MiB of HBM per device.

v0:
```python
import functools

import jax
import jax.numpy as jnp
from jax import lax
from jax.experimental import pallas as pl
from jax.experimental.pallas import tpu as pltpu
from jax.sharding import PartitionSpec as P

QUERY_HEADS = 64
KEY_VALUE_HEADS = 8
HEAD_SIZE = 128
BLOCK_TOKENS = 128
LOCAL_BAND_SIZE = 4
PICKED_BLOCKS = 2
GROUP = QUERY_HEADS // KEY_VALUE_HEADS

rope_base = 500000.0
masked_score = -1e30
log2_e = 1.4426950408889634


def from_behind(block, axis, distance):
    devices = range(lax.axis_size(axis))
    route = [(i - distance, i) for i in devices if i - distance in devices]
    return lax.ppermute(block, axis, route)


def rotate(x, cosine, sine):
    wide = x.astype(jnp.float32)
    return wide * cosine + pltpu.roll(wide, HEAD_SIZE // 2, 1) * sine


def kv_kernel(keys, values, cosine, sine, kv):
    for head in range(KEY_VALUE_HEADS):
        columns = slice(head * HEAD_SIZE, (head + 1) * HEAD_SIZE)
        kv[0, head, 0] = rotate(keys[:, columns], cosine[...], sine[...]).astype(jnp.bfloat16)
        kv[0, head, 1] = values[:, columns]


def dot_nt(a, b):
    return lax.dot_general(a, b, (((1,), (1,)), ((), ())), preferred_element_type=jnp.float32)


def with_ones(v):
    return jnp.concatenate([v, jnp.ones_like(v)], 1)


def band_kernel(blocks, me, queries, cosine, sine, far, near, own, rotated, partial, stats):
    k_all = jnp.concatenate([far[0, 0]] + [near[i, 0, 0] for i in range(blocks)] + [own[i, 0, 0] for i in range(blocks)], 0)
    v_all = with_ones(
        jnp.concatenate([far[0, 1]] + [near[i, 0, 1] for i in range(blocks)] + [own[i, 0, 1] for i in range(blocks)], 0)
    )
    width = LOCAL_BAND_SIZE * BLOCK_TOKENS
    row = lax.broadcasted_iota(jnp.int32, (BLOCK_TOKENS, width), 0)
    column = lax.broadcasted_iota(jnp.int32, (BLOCK_TOKENS, width), 1)
    lane = lax.broadcasted_iota(jnp.int32, (BLOCK_TOKENS, 128), 1)
    for i in range(blocks):
        first = (me[0] * blocks + i - (LOCAL_BAND_SIZE - 1)) * BLOCK_TOKENS
        good = (column <= row + (LOCAL_BAND_SIZE - 1) * BLOCK_TOKENS) & (column + first >= 0)
        bias = jnp.where(good, 0.0, masked_score)
        k = k_all[i * BLOCK_TOKENS : i * BLOCK_TOKENS + width]
        v = v_all[i * BLOCK_TOKENS : i * BLOCK_TOKENS + width]
        rows = slice(i * BLOCK_TOKENS, (i + 1) * BLOCK_TOKENS)
        held = jnp.zeros((BLOCK_TOKENS, 128), jnp.float32)
        for n in range(GROUP):
            columns = slice(n * HEAD_SIZE, (n + 1) * HEAD_SIZE)
            q = rotate(queries[rows, columns], cosine[rows], sine[rows]).astype(jnp.bfloat16)
            rotated[rows, columns] = q
            score = dot_nt(q, k) + bias
            top = jnp.max(score, 1, keepdims=True)
            weight = jnp.exp2(score - top).astype(jnp.bfloat16)
            summed = jnp.dot(weight, v, preferred_element_type=jnp.float32)
            total = summed[:, HEAD_SIZE:]
            partial[rows, columns] = (summed[:, :HEAD_SIZE] / total).astype(jnp.bfloat16)
            held = jnp.where(lane == n, top + jnp.log2(total), held)
        stats[0, rows] = held


def pick_kernel(blocks, slots, live, rotated, partial, stats, *rest):
    landed, out = rest[:-1], rest[-1]
    head = pl.program_id(0)
    column = lax.broadcasted_iota(jnp.int32, (1, PICKED_BLOCKS * BLOCK_TOKENS), 1)
    for i in range(blocks):
        pair = landed[i * PICKED_BLOCKS : (i + 1) * PICKED_BLOCKS]
        k = jnp.concatenate([p[0, 0] for p in pair], 0)
        v = with_ones(jnp.concatenate([p[0, 1] for p in pair], 0))
        bias = jnp.zeros(column.shape, jnp.float32)
        for p in range(PICKED_BLOCKS):
            at = (i * KEY_VALUE_HEADS + head) * PICKED_BLOCKS + p
            gone = jnp.where(live[at] > 0, 0.0, masked_score)
            bias = jnp.where(column // BLOCK_TOKENS == p, gone, bias)
        rows = slice(i * BLOCK_TOKENS, (i + 1) * BLOCK_TOKENS)
        for n in range(GROUP):
            columns = slice(n * HEAD_SIZE, (n + 1) * HEAD_SIZE)
            score = dot_nt(rotated[rows, columns], k) + bias
            near_top = stats[0, rows, n : n + 1]
            top = jnp.maximum(jnp.max(score, 1, keepdims=True), near_top)
            weight = jnp.exp2(score - top).astype(jnp.bfloat16)
            summed = jnp.dot(weight, v, preferred_element_type=jnp.float32)
            near_weight = jnp.exp2(near_top - top)
            result = (partial[rows, columns].astype(jnp.float32) * near_weight + summed[:, :HEAD_SIZE]) / (
                near_weight + summed[:, HEAD_SIZE:]
            )
            out[rows, columns] = result.astype(jnp.bfloat16)


def shards(queries, keys, values, positions, picks):
    tokens = queries.shape[0]
    blocks = tokens // BLOCK_TOKENS
    window = lax.axis_size("ctx")
    me = lax.axis_index("ctx")
    cap = max(1, blocks * KEY_VALUE_HEADS * PICKED_BLOCKS // window)
    entry_dims = (2, BLOCK_TOKENS, HEAD_SIZE)
    per_head = GROUP * HEAD_SIZE

    half = HEAD_SIZE // 2
    freq = rope_base ** (-(jnp.arange(half, dtype=jnp.float32) * 2.0) / HEAD_SIZE)
    angle = positions.astype(jnp.float32)[:, None] * freq[None, :]
    cosine, sine = jnp.cos(angle), jnp.sin(angle)
    cosine = jnp.concatenate([cosine, cosine], 1)
    sine = jnp.concatenate([-sine, sine], 1)
    factor = HEAD_SIZE**-0.5 * log2_e

    row_spec = pl.BlockSpec((BLOCK_TOKENS, KEY_VALUE_HEADS * HEAD_SIZE), lambda i: (i, 0))
    angle_spec = pl.BlockSpec((BLOCK_TOKENS, HEAD_SIZE), lambda i: (i, 0))
    kv = pl.pallas_call(
        kv_kernel,
        grid=(blocks,),
        in_specs=[row_spec, row_spec, angle_spec, angle_spec],
        out_specs=pl.BlockSpec((1, KEY_VALUE_HEADS) + entry_dims, lambda i: (i, 0, 0, 0, 0)),
        out_shape=jax.ShapeDtypeStruct((blocks, KEY_VALUE_HEADS) + entry_dims, jnp.bfloat16),
        name="rotate_keys",
    )(keys, values, cosine, sine)

    near = from_behind(kv, "ctx", 1)
    far = from_behind(kv[blocks - 1], "ctx", 2)

    flat = picks.reshape(-1)
    count = flat.shape[0]
    live = flat >= 0
    index = jnp.maximum(flat, 0)
    owner = index // blocks
    order = jnp.arange(count, dtype=jnp.int32)
    entry = index % blocks * KEY_VALUE_HEADS + order // PICKED_BLOCKS % KEY_VALUE_HEADS
    same = live[:, None] & live[None, :] & (owner[:, None] == owner[None, :]) & (order[None, :] < order[:, None])
    rank = jnp.sum(same.astype(jnp.int32), axis=1)
    target = owner * cap + rank
    slot_ids = jnp.arange(window * cap, dtype=jnp.int32)
    hits = (target[:, None] == slot_ids[None, :]) & live[:, None]
    table = jnp.sum(jnp.where(hits, entry[:, None], 0), axis=0).reshape(window, cap)
    wanted = lax.all_to_all(table, "ctx", split_axis=0, concat_axis=0, tiled=True)
    answers = kv.reshape((blocks * KEY_VALUE_HEADS,) + entry_dims)[wanted.reshape(-1)]
    landed = lax.all_to_all(answers, "ctx", split_axis=0, concat_axis=0, tiled=True)
    slots = owner * cap + jnp.minimum(rank, cap - 1)

    all_rows = pl.BlockSpec((tokens, HEAD_SIZE), lambda h: (0, 0))
    head_columns = pl.BlockSpec((tokens, per_head), lambda h: (0, h))
    head_blocks = pl.BlockSpec((blocks, 1) + entry_dims, lambda h: (0, h, 0, 0, 0))
    stats_spec = pl.BlockSpec((1, tokens, 128), lambda h: (h, 0, 0))
    limit = pltpu.CompilerParams(vmem_limit_bytes=32 * 1024 * 1024)
    width = LOCAL_BAND_SIZE * BLOCK_TOKENS
    rotated, partial, stats = pl.pallas_call(
        functools.partial(band_kernel, blocks),
        grid=(KEY_VALUE_HEADS,),
        in_specs=[
            pl.BlockSpec(memory_space=pltpu.SMEM),
            head_columns,
            all_rows,
            all_rows,
            pl.BlockSpec((1,) + entry_dims, lambda h: (h, 0, 0, 0)),
            head_blocks,
            head_blocks,
        ],
        out_specs=[head_columns, head_columns, stats_spec],
        out_shape=[
            jax.ShapeDtypeStruct(queries.shape, jnp.bfloat16),
            jax.ShapeDtypeStruct(queries.shape, jnp.bfloat16),
            jax.ShapeDtypeStruct((KEY_VALUE_HEADS, tokens, 128), jnp.float32),
        ],
        compiler_params=limit,
        cost_estimate=pl.CostEstimate(
            flops=4 * tokens * QUERY_HEADS * HEAD_SIZE * width * 2,
            bytes_accessed=tokens * QUERY_HEADS * HEAD_SIZE * 6,
            transcendentals=tokens * QUERY_HEADS * width,
        ),
        name="band_attention",
    )(me.reshape(1), queries, cosine * factor, sine * factor, far, near, kv)

    def slot_spec(i, p):
        def place(h, slot, alive):
            return (slot[(i * KEY_VALUE_HEADS + h) * PICKED_BLOCKS + p], 0, 0, 0)

        return pl.BlockSpec((1,) + entry_dims, place)

    head_columns = pl.BlockSpec((tokens, per_head), lambda h, *_: (0, h))
    return pl.pallas_call(
        functools.partial(pick_kernel, blocks),
        grid_spec=pltpu.PrefetchScalarGridSpec(
            num_scalar_prefetch=2,
            grid=(KEY_VALUE_HEADS,),
            in_specs=[head_columns, head_columns, pl.BlockSpec((1, tokens, 128), lambda h, *_: (h, 0, 0))]
            + [slot_spec(i, p) for i in range(blocks) for p in range(PICKED_BLOCKS)],
            out_specs=head_columns,
        ),
        out_shape=jax.ShapeDtypeStruct(queries.shape, jnp.bfloat16),
        compiler_params=limit,
        name="picked_attention",
    )(slots, live.astype(jnp.int32), rotated, partial, stats, *[landed] * (blocks * PICKED_BLOCKS))


def solution(mesh):
    rows = P(("groups", "ctx"), None)
    return jax.shard_map(
        shards,
        mesh=mesh,
        in_specs=(rows, rows, rows, P(("groups", "ctx")), P(("groups", "ctx"), None, None)),
        out_specs=rows,
        check_vma=False,
    )
```

profile of v0, /device:TPU:17, one launch (start us, length us, event | category | flops | bytes accessed | tf_op | source)
XLA Modules:
  0.0 146.0 jit_solution(7213677449679618633)
XLA Ops:
  0.0 0.7 broadcast_compare_fusion
  0.7 0.7 maximum_and_fusion
  1.4 0.1 copy.22
  1.5 0.1 ge.15
  1.6 0.1 copy.19
  1.7 0.1 ne.86
  1.8 0.1 copy.20
  1.9 0.1 rem.37
  2.0 0.1 copy.21
  2.0 0.1 div.19
  2.2 0.2 convert_reduce_fusion
  2.4 0.1 select_reduce_fusion
  2.5 0.7 all_to_all.9
  3.1 6.5 %all-to-all-start = ((s32[16,1,2]{2,1,0:T(1,128)}), s32[16,1,2]{2,1,0:T(1,128)S(1)}, u32[]{:S(2)}, u32[]{:S(2)}) async-start(s32[16,1,2]{2,1,0:T(1,128)} %bitcast.3), calls=%async_computation | async-start | bytes 16384 | tf_op jit(solution)/shard_map/all_to_all | solution.py:152
  9.6 0.7 convert_element_type.11
  10.3 0.5 fusion
  10.8 0.8 pad_maximum_fusion
  11.7 2.2 %rotate_keys.1.own = bf16[2,8,2,128,128]{4,3,2,1,0:T(8,128)(2,1)} custom-call(bf16[256,1024]{1,0:T(8,128)(2,1)} %keys.1, bf16[256,1024]{1,0:T(8,128)(2,1)} %values.1, f32[256,128]{1,0:T(8,128)} %get-tuple-element.13.cosine, f32[256,128]{1,0:T(8,128)} %get-tuple-element.27.sine), custom_call_target="tpu_custom_call" | custom-call | tf_op jit(solution)/shard_map/rotate_keys/pallas_call | solution.py:127
  13.9 0.0 all-to-all-done
  13.9 0.5 broadcast.248
  14.5 0.7 reduce.3
  15.1 0.1 reshape.142
  15.2 3.4 %gather_fusion = bf16[32,2,128,128]{3,2,1,0:T(8,128)(2,1)} fusion(bf16[16,2,128,128]{3,2,1,0:T(8,128)(2,1)} %bitcast.7, s32[1024]{0:T(1024)S(1)} %pad_clamp_fusion), kind=kCustom, calls=%fused_computation | custom fusion | bytes 4194432 | tf_op jit(solution)/shard_map/gather | solution.py:153
  18.6 0.0 copy-start
  18.6 6.1 %all-to-all-start.1 = ((bf16[32,2,128,128]{3,2,1,0:T(8,128)(2,1)}), bf16[32,2,128,128]{3,2,1,0:T(8,128)(2,1)S(1)}, u32[]{:S(2)}, u32[]{:S(2)}) async-start(bf16[32,2,128,128]{3,2,1,0:T(8,128)(2,1)} %gather_fusion), calls=%async_computation.1 | async-start | bytes 4194304 | tf_op jit(solution)/shard_map/all_to_all | solution.py:154
  24.8 0.0 copy-done
  24.8 3.3 %collective-permute-start.1 = (bf16[2,8,2,128,128]{4,3,2,1,0:T(8,128)(2,1)S(1)}, bf16[2,8,2,128,128]{4,3,2,1,0:T(8,128)(2,1)}, u32[]{:S(2)}, u32[]{:S(2)}) collective-permute-start(bf16[2,8,2,128,128]{4,3,2,1,0:T(8,128)(2,1)S(1)} %copy-done), channel_id=1, source_target_pairs={{0,1},{1,2},{2,3},{3,4},{4,5},{5,6},{6,7},{7,8},{8,9},{9,10},{10,1... | collective-permute-start | bytes 3145736 | tf_op jit(solution)/shard_map/ppermute | solution.py:26
  28.1 0.8 slice_bitcast_fusion
  28.9 3.1 %collective-permute-start = (bf16[8,2,128,128]{3,2,1,0:T(8,128)(2,1)}, bf16[8,2,128,128]{3,2,1,0:T(8,128)(2,1)}, u32[]{:S(2)}, u32[]{:S(2)}) collective-permute-start(bf16[8,2,128,128]{3,2,1,0:T(8,128)(2,1)} %slice_bitcast_fusion), channel_id=1, source_target_pairs={{0,2},{1,3},{2,4},{3,5},{4,6},{5,7},{6,8},{7,9},{8,10},{9,11},{10,... | collective-permute-start | bytes 1572872 | tf_op jit(solution)/shard_map/ppermute | solution.py:26
  32.0 62.6 %collective-permute-done.far = bf16[8,2,128,128]{3,2,1,0:T(8,128)(2,1)} collective-permute-done((bf16[8,2,128,128]{3,2,1,0:T(8,128)(2,1)}, bf16[8,2,128,128]{3,2,1,0:T(8,128)(2,1)}, u32[]{:S(2)}, u32[]{:S(2)}) %collective-permute-start) | collective-permute-done | bytes 524320 | tf_op jit(solution)/shard_map/ppermute | solution.py:26
  94.7 0.0 collective-permute-done.1.near
  94.7 0.0 copy-start.7
  94.7 2.2 %copy-done.7 = bf16[256,8192]{1,0:T(8,128)(2,1)S(1)} copy-done((bf16[256,8192]{1,0:T(8,128)(2,1)S(1)}, bf16[256,8192]{1,0:T(8,128)(2,1)}, u32[]{:S(2)}) %copy-start.7) | copy-done | bytes 4194328
  96.9 16.5 %band_attention.1 = (bf16[256,8192]{1,0:T(8,128)(2,1)S(1)}, bf16[256,8192]{1,0:T(8,128)(2,1)S(1)}, f32[8,256,128]{2,1,0:T(8,128)S(1)}) custom-call(s32[1]{0:T(128)} %bitcast.me, bf16[256,8192]{1,0:T(8,128)(2,1)S(1)} %copy-done.7, f32[256,128]{1,0:T(8,128)S(1)} %get-tuple-element.14.cosine, f32[256,128]{1,0:T(8,128)S(1)} %get-tuple-element.26.sine, ...), custom_call_target="tpu_custom_call" | custom-call | flops 8589934592 | bytes 12582912 | tf_op jit(solution)/shard_map/band_attention/pallas_call | solution.py:163
  113.4 0.0 copy-start.1
  113.4 2.0 %copy-done.1 = bf16[256,8192]{1,0:T(8,128)(2,1)} copy-done((bf16[256,8192]{1,0:T(8,128)(2,1)}, bf16[256,8192]{1,0:T(8,128)(2,1)S(1)}, u32[]{:S(2)}) %copy-start.1) | copy-done | bytes 4194328
  115.4 0.0 copy-start.3
  115.4 1.9 %copy-done.3 = bf16[256,8192]{1,0:T(8,128)(2,1)} copy-done((bf16[256,8192]{1,0:T(8,128)(2,1)}, bf16[256,8192]{1,0:T(8,128)(2,1)S(1)}, u32[]{:S(2)}) %copy-start.3) | copy-done | bytes 4194328
  117.4 0.0 copy-start.5
  117.4 1.0 copy-done.5
  118.4 0.0 all-to-all-done.1.rest_0_.rest_1_.rest_2_.rest_3_
  118.4 0.0 copy-start.2
  118.4 2.2 %copy-done.2 = bf16[256,8192]{1,0:T(8,128)(2,1)S(1)} copy-done((bf16[256,8192]{1,0:T(8,128)(2,1)S(1)}, bf16[256,8192]{1,0:T(8,128)(2,1)}, u32[]{:S(2)}) %copy-start.2) | copy-done | bytes 4194328
  120.6 0.0 copy-start.4
  120.6 2.2 %copy-done.4 = bf16[256,8192]{1,0:T(8,128)(2,1)S(1)} copy-done((bf16[256,8192]{1,0:T(8,128)(2,1)S(1)}, bf16[256,8192]{1,0:T(8,128)(2,1)}, u32[]{:S(2)}) %copy-start.4) | copy-done | bytes 4194328
  122.8 0.0 copy-start.6
  122.8 1.2 copy-done.6
  124.0 22.0 %picked_attention.1 = bf16[256,8192]{1,0:T(8,128)(2,1)} custom-call(s32[32]{0:T(128)S(1)} %get-tuple-element.23.slots, s32[32]{0:T(128)S(1)} %convert_element_type.10.live, bf16[256,8192]{1,0:T(8,128)(2,1)S(1)} %copy-done.2, bf16[256,8192]{1,0:T(8,128)(2,1)S(1)} %copy-done.4, f32[8,256,128]{2,1,0:T(8,128)S(1)} %copy-done.6, ...), custom_call_target="tpu_custom_call" | custom-call | tf_op jit(solution)/shard_map/picked_attention/pallas_call | solution.py:197
  (6 shorter events, 0.0 us)
Async XLA Ops:
  3.1 10.8 %all-to-all-start = ((s32[16,1,2]{2,1,0:T(1,128)}), s32[16,1,2]{2,1,0:T(1,128)S(1)}, u32[]{:S(2)}, u32[]{:S(2)}) async-start(s32[16,1,2]{2,1,0:T(1,128)} %bitcast.3), calls=%async_computation | async-start | bytes 16384 | tf_op jit(solution)/shard_map/all_to_all | solution.py:152
  18.6 6.2 %copy-start = (bf16[2,8,2,128,128]{4,3,2,1,0:T(8,128)(2,1)S(1)}, bf16[2,8,2,128,128]{4,3,2,1,0:T(8,128)(2,1)}, u32[]{:S(2)}) copy-start(bf16[2,8,2,128,128]{4,3,2,1,0:T(8,128)(2,1)} %rotate_keys.1.own) | copy-start | bytes 3145732
  18.6 99.8 %all-to-all-start.1 = ((bf16[32,2,128,128]{3,2,1,0:T(8,128)(2,1)}), bf16[32,2,128,128]{3,2,1,0:T(8,128)(2,1)S(1)}, u32[]{:S(2)}, u32[]{:S(2)}) async-start(bf16[32,2,128,128]{3,2,1,0:T(8,128)(2,1)} %gather_fusion), calls=%async_computation.1 | async-start | bytes 4194304 | tf_op jit(solution)/shard_map/all_to_all | solution.py:154
  24.8 69.9 %collective-permute-start.1 = (bf16[2,8,2,128,128]{4,3,2,1,0:T(8,128)(2,1)S(1)}, bf16[2,8,2,128,128]{4,3,2,1,0:T(8,128)(2,1)}, u32[]{:S(2)}, u32[]{:S(2)}) collective-permute-start(bf16[2,8,2,128,128]{4,3,2,1,0:T(8,128)(2,1)S(1)} %copy-done), channel_id=1, source_target_pairs={{0,1},{1,2},{2,3},{3,4},{4,5},{5,6},{6,7},{7,8},{8,9},{9,10},{10,1... | collective-permute-start | bytes 3145736 | tf_op jit(solution)/shard_map/ppermute | solution.py:26
  28.9 65.8 %collective-permute-start = (bf16[8,2,128,128]{3,2,1,0:T(8,128)(2,1)}, bf16[8,2,128,128]{3,2,1,0:T(8,128)(2,1)}, u32[]{:S(2)}, u32[]{:S(2)}) collective-permute-start(bf16[8,2,128,128]{3,2,1,0:T(8,128)(2,1)} %slice_bitcast_fusion), channel_id=1, source_target_pairs={{0,2},{1,3},{2,4},{3,5},{4,6},{5,7},{6,8},{7,9},{8,10},{9,11},{10,... | collective-permute-start | bytes 1572872 | tf_op jit(solution)/shard_map/ppermute | solution.py:26
  94.7 2.2 %copy-start.7 = (bf16[256,8192]{1,0:T(8,128)(2,1)S(1)}, bf16[256,8192]{1,0:T(8,128)(2,1)}, u32[]{:S(2)}) copy-start(bf16[256,8192]{1,0:T(8,128)(2,1)} %queries.1) | copy-start | bytes 12582916
  113.4 2.0 %copy-start.1 = (bf16[256,8192]{1,0:T(8,128)(2,1)}, bf16[256,8192]{1,0:T(8,128)(2,1)S(1)}, u32[]{:S(2)}) copy-start(bf16[256,8192]{1,0:T(8,128)(2,1)S(1)} %get-tuple-element.8.rotated) | copy-start | bytes 12582916
  115.4 2.0 %copy-start.3 = (bf16[256,8192]{1,0:T(8,128)(2,1)}, bf16[256,8192]{1,0:T(8,128)(2,1)S(1)}, u32[]{:S(2)}) copy-start(bf16[256,8192]{1,0:T(8,128)(2,1)S(1)} %get-tuple-element.9.partial) | copy-start | bytes 12582916
  117.4 1.0 copy-start.5
  118.4 2.2 %copy-start.2 = (bf16[256,8192]{1,0:T(8,128)(2,1)S(1)}, bf16[256,8192]{1,0:T(8,128)(2,1)}, u32[]{:S(2)}) copy-start(bf16[256,8192]{1,0:T(8,128)(2,1)} %copy-done.1) | copy-start | bytes 12582916
  120.6 2.2 %copy-start.4 = (bf16[256,8192]{1,0:T(8,128)(2,1)S(1)}, bf16[256,8192]{1,0:T(8,128)(2,1)}, u32[]{:S(2)}) copy-start(bf16[256,8192]{1,0:T(8,128)(2,1)} %copy-done.3) | copy-start | bytes 12582916
  122.8 1.2 copy-start.6
where the time goes:
time: 147 us; the launch traced here: 146 us
  waiting for transfers between devices  62.7 us (43%)
  Pallas kernels  40.8 us (28%)
  local copies, waits for them, and re-layouts  19 us (13%)
  starting transfers between devices  19 us (13%)
  other arithmetic  4.42 us (3%)
    ppermute x2, waiting for transfers between devices, from_behind(): return lax.ppermute(block, axis, route)  62.7 us
    pallas_call x1, Pallas kernels, shards(): pl.pallas_call(functools.partial(pick_kernel, blocks), grid_spec=pltpu.Pr...  22 us
    pallas_call x1, Pallas kernels, shards(): pl.pallas_call(functools.partial(band_kernel, blocks), grid=(KEY_VALUE_HE...  16.5 us
    unnamed x16, local copies, waits for them, and re-layouts  12.7 us
    all_to_all x1, starting transfers between devices, shards(): lax.all_to_all(table, 'ctx', split_axis=0, concat_axis=0, tiled=True)  6.47 us
    ppermute x2, starting transfers between devices, from_behind(): return lax.ppermute(block, axis, route)  6.42 us
    all_to_all x1, starting transfers between devices, shards(): lax.all_to_all(answers, 'ctx', split_axis=0, concat_axis=0, tiled=True)  6.15 us
    gather x1, local copies, waits for them, and re-layouts, shards(): kv.reshape((blocks * KEY_VALUE_HEADS,) + entry_dims)[wanted.reshape(-1)]  3.36 us
  transfers between devices with their start and end apart: 4, of which 1 were waited for; matrix products, arithmetic and copies ran while one was open for 2% of the time, Pallas kernels for 13%

commit v1 on v0

v1 whole, which is shorter than its diff:
```python
import functools

import jax
import jax.numpy as jnp
from jax import lax
from jax.experimental import pallas as pl
from jax.experimental.pallas import tpu as pltpu
from jax.sharding import PartitionSpec as P

QUERY_HEADS = 64
KEY_VALUE_HEADS = 8
HEAD_SIZE = 128
BLOCK_TOKENS = 128
LOCAL_BAND_SIZE = 4
PICKED_BLOCKS = 2
GROUP = QUERY_HEADS // KEY_VALUE_HEADS
ENTRY = (2, BLOCK_TOKENS, HEAD_SIZE)

rope_base = 500000.0
masked_score = -1e30
log2_e = 1.4426950408889634


def rotate(x, cosine, sine):
    wide = x.astype(jnp.float32)
    return wide * cosine + pltpu.roll(wide, HEAD_SIZE // 2, 1) * sine


def dot_nt(a, b):
    return lax.dot_general(a, b, (((1,), (1,)), ((), ())), preferred_element_type=jnp.float32)


def with_ones(v):
    return jnp.concatenate([v, jnp.ones_like(v)], 1)


def stack_heads(x):
    return jnp.concatenate([x[:, n * HEAD_SIZE : (n + 1) * HEAD_SIZE] for n in range(GROUP)], 0)


def head_rows(n):
    return slice(n * BLOCK_TOKENS, (n + 1) * BLOCK_TOKENS)


def flip(a, b, size):
    out, bit = 0, 1
    while bit < size:
        out = out + (a // bit + b // bit) % 2 * bit
        bit *= 2
    return out


def exchange_kernel(
    blocks, window, cap,
    queries, keys, values, cosine, sine, pick_row, pick_column,
    rotated, partial, stats, landed, slots,
    q_held, rotated_held, partial_held, stats_held, kv, near, far, answers, request, requests, scalars,
    load_sem, store_sem, near_sem, far_sem, request_send, request_recv, scalar_sem, answer_send, answer_recv,
):
    me = lax.axis_index("ctx")
    count = pick_row.shape[1]
    per_head = GROUP * HEAD_SIZE
    barrier = pltpu.get_barrier_semaphore()

    def greet(j, carry):
        pl.semaphore_signal(barrier, inc=1, device_id={"ctx": lax.rem(me + j, window)})
        return carry

    lax.fori_loop(1, window, greet, 0)

    def load(h):
        columns = pl.ds(pl.multiple_of(h * per_head, per_head), per_head)
        return pltpu.make_async_copy(queries.at[:, columns], q_held.at[h], load_sem.at[h])

    def start_load(h, carry):
        load(h).start()
        return carry

    lax.fori_loop(0, KEY_VALUE_HEADS, start_load, 0)

    row, column = pick_row[...], pick_column[...]
    row_owner = jnp.maximum(row, 0) // blocks
    column_owner = jnp.maximum(column, 0) // blocks
    first = lax.broadcasted_iota(jnp.int32, (count, count), 0)
    second = lax.broadcasted_iota(jnp.int32, (count, count), 1)
    alike = (column_owner == row_owner) & (column >= 0) & (row >= 0)
    column_rank = jnp.sum((alike & (second < first)).astype(jnp.int32), 1, keepdims=True)
    row_rank = jnp.sum((alike & (first < second)).astype(jnp.int32), 0, keepdims=True)
    slots[...] = jnp.where(row >= 0, row_owner * cap + jnp.minimum(row_rank, cap - 1), -1)
    order = lax.broadcasted_iota(jnp.int32, (count, 1), 0)
    entry = jnp.maximum(column, 0) % blocks * KEY_VALUE_HEADS + order // PICKED_BLOCKS % KEY_VALUE_HEADS
    lane = lax.broadcasted_iota(jnp.int32, (count, request.shape[1]), 1)
    hit = (column_owner * cap + column_rank == lane) & (column >= 0)
    request[...] = jnp.sum(jnp.where(hit, entry, 0), 0, keepdims=True)

    for i in range(blocks):
        rows = slice(i * BLOCK_TOKENS, (i + 1) * BLOCK_TOKENS)
        for head in range(KEY_VALUE_HEADS):
            columns = slice(head * HEAD_SIZE, (head + 1) * HEAD_SIZE)
            kv[i * KEY_VALUE_HEADS + head, 0] = rotate(keys[rows, columns], cosine[rows], sine[rows]).astype(jnp.bfloat16)
            kv[i * KEY_VALUE_HEADS + head, 1] = values[rows, columns]

    @pl.when(me < 1)
    def _():
        near[...] = jnp.zeros_like(near)

    @pl.when(me < 2)
    def _():
        far[...] = jnp.zeros_like(far)

    pl.semaphore_wait(barrier, window - 1)

    def ask(owner):
        return pltpu.make_async_remote_copy(
            src_ref=request, dst_ref=requests.at[me], send_sem=request_send.at[owner], recv_sem=request_recv.at[me],
            device_id={"ctx": owner},
        )

    def asked(source):
        return pltpu.make_async_remote_copy(
            src_ref=request, dst_ref=requests.at[source], send_sem=request_send.at[source],
            recv_sem=request_recv.at[source], device_id={"ctx": source},
        )

    def start_ask(owner, carry):
        ask(owner).start()
        return carry

    lax.fori_loop(0, me, start_ask, 0)

    last = pl.ds((blocks - 1) * KEY_VALUE_HEADS, KEY_VALUE_HEADS)
    send_near = pltpu.make_async_remote_copy(
        src_ref=kv, dst_ref=near, send_sem=near_sem.at[0], recv_sem=near_sem.at[1],
        device_id={"ctx": lax.rem(me + 1, window)},
    )
    send_far = pltpu.make_async_remote_copy(
        src_ref=kv.at[last], dst_ref=far, send_sem=far_sem.at[0], recv_sem=far_sem.at[1],
        device_id={"ctx": lax.rem(me + 2, window)},
    )

    @pl.when(me + 1 < window)
    def _():
        send_near.start()

    @pl.when(me + 2 < window)
    def _():
        send_far.start()

    def await_request(source, carry):
        asked(source).wait_recv()
        return carry

    lax.fori_loop(me + 1, window, await_request, 0)
    to_scalars = pltpu.make_async_copy(requests, scalars, scalar_sem)
    to_scalars.start()
    to_scalars.wait()

    def answer(other, at, slot):
        return pltpu.make_async_remote_copy(
            src_ref=answers.at[at], dst_ref=landed.at[slot], send_sem=answer_send.at[at], recv_sem=answer_recv.at[slot],
            device_id={"ctx": other},
        )

    def start_answer(j, carry):
        other = flip(me, window - 1 - j, window)

        @pl.when(other > me)
        def _():
            for c in range(cap):
                answers[other, c] = kv[scalars[other, 0, me * cap + c]]
            answer(other, other, me).start()

        return carry

    lax.fori_loop(0, window - 1, start_answer, 0)

    @pl.when(me >= 1)
    def _():
        send_near.wait_recv()

    @pl.when(me >= 2)
    def _():
        send_far.wait_recv()

    width = LOCAL_BAND_SIZE * BLOCK_TOKENS
    factor = HEAD_SIZE**-0.5 * log2_e
    row = lax.broadcasted_iota(jnp.int32, (BLOCK_TOKENS, width), 0)
    column = lax.broadcasted_iota(jnp.int32, (BLOCK_TOKENS, width), 1)
    lane = lax.broadcasted_iota(jnp.int32, (BLOCK_TOKENS, 128), 1)

    def store(h):
        return [
            pltpu.make_async_copy(rotated_held.at[h], rotated.at[h], store_sem.at[0, h]),
            pltpu.make_async_copy(partial_held.at[h], partial.at[h], store_sem.at[1, h]),
            pltpu.make_async_copy(stats_held.at[h], stats.at[h], store_sem.at[2, h]),
        ]

    def one_head(h, carry):
        load(h).wait()
        band = [far[h]] + [near[i * KEY_VALUE_HEADS + h] for i in range(blocks)]
        band = band + [kv[i * KEY_VALUE_HEADS + h] for i in range(blocks)]
        k_all = jnp.concatenate([b[0] for b in band], 0)
        v_all = with_ones(jnp.concatenate([b[1] for b in band], 0))
        for i in range(blocks):
            start = (me * blocks + i - (LOCAL_BAND_SIZE - 1)) * BLOCK_TOKENS
            good = (column <= row + (LOCAL_BAND_SIZE - 1) * BLOCK_TOKENS) & (column + start >= 0)
            bias = jnp.where(good, 0.0, masked_score)
            rows = slice(i * BLOCK_TOKENS, (i + 1) * BLOCK_TOKENS)
            k = k_all[i * BLOCK_TOKENS : i * BLOCK_TOKENS + width]
            v = v_all[i * BLOCK_TOKENS : i * BLOCK_TOKENS + width]
            q_cosine, q_sine = cosine[rows] * factor, sine[rows] * factor
            held = jnp.zeros((BLOCK_TOKENS, 128), jnp.float32)
            for n in range(GROUP):
                columns = slice(n * HEAD_SIZE, (n + 1) * HEAD_SIZE)
                q = rotate(q_held[h, rows, columns], q_cosine, q_sine).astype(jnp.bfloat16)
                rotated_held[h, rows, columns] = q
                score = dot_nt(q, k) + bias
                top = jnp.max(score, 1, keepdims=True)
                weight = jnp.exp2(score - top).astype(jnp.bfloat16)
                summed = jnp.dot(weight, v, preferred_element_type=jnp.float32)
                total = summed[:, HEAD_SIZE:]
                partial_held[h, rows, columns] = (summed[:, :HEAD_SIZE] / total).astype(jnp.bfloat16)
                held = jnp.where(lane == n, top + jnp.log2(total), held)
            stats_held[h, rows] = held
        for copy in store(h):
            copy.start()
        return carry

    lax.fori_loop(0, KEY_VALUE_HEADS, one_head, 0)

    def end_store(h, carry):
        for copy in store(h):
            copy.wait()
        return carry

    lax.fori_loop(0, KEY_VALUE_HEADS, end_store, 0)

    @pl.when(me + 1 < window)
    def _():
        send_near.wait_send()

    @pl.when(me + 2 < window)
    def _():
        send_far.wait_send()

    def end_ask(owner, carry):
        ask(owner).wait_send()
        return carry

    lax.fori_loop(0, me, end_ask, 0)

    def end_answer(other, carry):
        answer(other, other, me).wait_send()
        return carry

    lax.fori_loop(me + 1, window, end_answer, 0)

    def arrive(source, carry):
        answer(source, source, source).wait_recv()
        return carry

    lax.fori_loop(0, me, arrive, 0)


def pick_kernel(blocks, slots, rotated, partial, stats, *rest):
    landed, out = rest[:-1], rest[-1]
    head = pl.program_id(0)
    column = lax.broadcasted_iota(jnp.int32, (1, PICKED_BLOCKS * BLOCK_TOKENS), 1)
    for i in range(blocks):
        ks, vs = [], []
        bias = jnp.zeros(column.shape, jnp.float32)
        for p in range(PICKED_BLOCKS):
            at = (i * KEY_VALUE_HEADS + head) * PICKED_BLOCKS + p
            alive = slots[0, at] >= 0
            pair = landed[i * PICKED_BLOCKS + p]
            ks.append(jnp.where(alive, pair[0, 0], jnp.zeros_like(pair[0, 0])))
            vs.append(jnp.where(alive, pair[0, 1], jnp.zeros_like(pair[0, 1])))
            bias = jnp.where(column // BLOCK_TOKENS == p, jnp.where(alive, 0.0, masked_score), bias)
        k = jnp.concatenate(ks, 0)
        v = with_ones(jnp.concatenate(vs, 0))
        rows = slice(i * BLOCK_TOKENS, (i + 1) * BLOCK_TOKENS)
        score = dot_nt(stack_heads(rotated[0, rows]), k) + bias
        near_top = jnp.concatenate([stats[0, rows, n : n + 1] for n in range(GROUP)], 0)
        top = jnp.maximum(jnp.max(score, 1, keepdims=True), near_top)
        weight = jnp.exp2(score - top).astype(jnp.bfloat16)
        summed = jnp.dot(weight, v, preferred_element_type=jnp.float32)
        near_weight = jnp.exp2(near_top - top)
        held = stack_heads(partial[0, rows]).astype(jnp.float32)
        result = (held * near_weight + summed[:, :HEAD_SIZE]) / (near_weight + summed[:, HEAD_SIZE:])
        result = result.astype(jnp.bfloat16)
        for n in range(GROUP):
            out[rows, n * HEAD_SIZE : (n + 1) * HEAD_SIZE] = result[head_rows(n)]


def shards(queries, keys, values, positions, picks):
    tokens = queries.shape[0]
    blocks = tokens // BLOCK_TOKENS
    window = lax.axis_size("ctx")
    cap = max(1, blocks * KEY_VALUE_HEADS * PICKED_BLOCKS // window)
    per_head = GROUP * HEAD_SIZE
    entries = blocks * KEY_VALUE_HEADS
    count = entries * PICKED_BLOCKS
    lanes = -(-window * cap // 128) * 128

    half = HEAD_SIZE // 2
    freq = rope_base ** (-(jnp.arange(half, dtype=jnp.float32) * 2.0) / HEAD_SIZE)
    angle = positions.astype(jnp.float32)[:, None] * freq[None, :]
    cosine, sine = jnp.cos(angle), jnp.sin(angle)
    cosine = jnp.concatenate([cosine, cosine], 1)
    sine = jnp.concatenate([-sine, sine], 1)

    here = pl.BlockSpec(memory_space=pltpu.VMEM)
    there = pl.BlockSpec(memory_space=pl.ANY)
    by_head = (KEY_VALUE_HEADS, tokens, per_head)
    stats_dims = (KEY_VALUE_HEADS, tokens, 128)
    width = LOCAL_BAND_SIZE * BLOCK_TOKENS
    limit = 56 * 1024 * 1024
    rotated, partial, stats, landed, slots = pl.pallas_call(
        functools.partial(exchange_kernel, blocks, window, cap),
        in_specs=[there] + [here] * 6,
        out_specs=[there] * 4 + [here],
        out_shape=[
            jax.ShapeDtypeStruct(by_head, jnp.bfloat16),
            jax.ShapeDtypeStruct(by_head, jnp.bfloat16),
            jax.ShapeDtypeStruct(stats_dims, jnp.float32),
            jax.ShapeDtypeStruct((window, cap) + ENTRY, jnp.bfloat16),
            jax.ShapeDtypeStruct((1, count), jnp.int32),
        ],
        scratch_shapes=[
            pltpu.VMEM(by_head, jnp.bfloat16),
            pltpu.VMEM(by_head, jnp.bfloat16),
            pltpu.VMEM(by_head, jnp.bfloat16),
            pltpu.VMEM(stats_dims, jnp.float32),
            pltpu.VMEM((entries,) + ENTRY, jnp.bfloat16),
            pltpu.VMEM((entries,) + ENTRY, jnp.bfloat16),
            pltpu.VMEM((KEY_VALUE_HEADS,) + ENTRY, jnp.bfloat16),
            pltpu.VMEM((window, cap) + ENTRY, jnp.bfloat16),
            pltpu.VMEM((1, lanes), jnp.int32),
            pltpu.VMEM((window, 1, lanes), jnp.int32),
            pltpu.SMEM((window, 1, lanes), jnp.int32),
            pltpu.SemaphoreType.DMA((KEY_VALUE_HEADS,)),
            pltpu.SemaphoreType.DMA((3, KEY_VALUE_HEADS)),
            pltpu.SemaphoreType.DMA((2,)),
            pltpu.SemaphoreType.DMA((2,)),
            pltpu.SemaphoreType.DMA((window,)),
            pltpu.SemaphoreType.DMA((window,)),
            pltpu.SemaphoreType.DMA,
            pltpu.SemaphoreType.DMA((window,)),
            pltpu.SemaphoreType.DMA((window,)),
        ],
        compiler_params=pltpu.CompilerParams(collective_id=0, has_side_effects=True, vmem_limit_bytes=limit),
        cost_estimate=pl.CostEstimate(
            flops=4 * tokens * QUERY_HEADS * HEAD_SIZE * width,
            bytes_accessed=tokens * QUERY_HEADS * HEAD_SIZE * 6,
            transcendentals=tokens * QUERY_HEADS * width,
        ),
        name="exchange_and_band",
    )(queries, keys, values, cosine, sine, picks.reshape(1, count), picks.reshape(count, 1))

    def slot_spec(i, p):
        def place(h, slot):
            return (jnp.maximum(slot[0, (i * KEY_VALUE_HEADS + h) * PICKED_BLOCKS + p], 0), 0, 0, 0)

        return pl.BlockSpec((1,) + ENTRY, place)

    by_head_spec = pl.BlockSpec((1, tokens, per_head), lambda h, *_: (h, 0, 0))
    landed = landed.reshape((window * cap,) + ENTRY)
    return pl.pallas_call(
        functools.partial(pick_kernel, blocks),
        grid_spec=pltpu.PrefetchScalarGridSpec(
            num_scalar_prefetch=1,
            grid=(KEY_VALUE_HEADS,),
            in_specs=[by_head_spec, by_head_spec, pl.BlockSpec((1, tokens, 128), lambda h, *_: (h, 0, 0))]
            + [slot_spec(i, p) for i in range(blocks) for p in range(PICKED_BLOCKS)],
            out_specs=pl.BlockSpec((tokens, per_head), lambda h, *_: (0, h)),
        ),
        out_shape=jax.ShapeDtypeStruct(queries.shape, jnp.bfloat16),
        compiler_params=pltpu.CompilerParams(vmem_limit_bytes=limit),
        name="picked_attention",
    )(slots, rotated, partial, stats, *[landed] * (blocks * PICKED_BLOCKS))


def solution(mesh):
    rows = P(("groups", "ctx"), None)
    return jax.shard_map(
        shards,
        mesh=mesh,
        in_specs=(rows, rows, rows, P(("groups", "ctx")), P(("groups", "ctx"), None, None)),
        out_specs=rows,
        check_vma=False,
    )
```

time: 147 us -> 107 us (0.73)
  waiting for transfers between devices: 62.7 us -> 0 us
  Pallas kernels: 40.8 us -> 103 us
  starting transfers between devices: 19 us -> 0 us
  local copies, waits for them, and re-layouts: 19 us -> 2.12 us
  other arithmetic: 4.42 us -> 2.05 us
    ppermute x2 -> x0, waiting for transfers between devices: 62.7 us -> none  [from_behind(): return lax.ppermute(block, axis, route)]
    pallas_call x2 -> x1, Pallas kernels: 18.8 us -> 78.8 us  [shards(): pl.pallas_call(functools.partial(exchange_kernel, blocks, window, cap), i...]
    all_to_all x2 -> x0, starting transfers between devices: 12.6 us -> none  [the longest x1 6.47 us: shards(): lax.all_to_all(table, 'ctx', split_axis=0, concat_axis=0, tiled=True)]
    unnamed x16 -> x1, local copies, waits for them, and re-layouts: 12.7 us -> 0.76 us
    ppermute x2 -> x0, starting transfers between devices: 6.42 us -> none  [from_behind(): return lax.ppermute(block, axis, route)]
    gather x1 -> x0, local copies, waits for them, and re-layouts: 3.36 us -> none  [shards(): kv.reshape((blocks * KEY_VALUE_HEADS,) + entry_dims)[wanted.reshape(-1)]]
    pallas_call x1, Pallas kernels: 22 us -> 23.9 us  [shards(): pl.pallas_call(functools.partial(pick_kernel, blocks), grid_spec=pltpu.Pr...]
  transfers between devices with their start and end apart: 4 -> 0, of which waited for: 1 -> 0; matrix products, arithmetic and copies ran while one was open for 2% -> 0% of each run, Pallas kernels for 13% -> 0%
where the time goes in v1:
time: 107 us
  Pallas kernels  103 us (96%)
  local copies, waits for them, and re-layouts  2.12 us (2%)
  other arithmetic  2.05 us (2%)
    pallas_call x1, Pallas kernels, shards(): pl.pallas_call(functools.partial(exchange_kernel, blocks, window, cap), i...  78.8 us
    pallas_call x1, Pallas kernels, shards(): pl.pallas_call(functools.partial(pick_kernel, blocks), grid_spec=pltpu.Pr...  23.9 us

profile of v1, /device:TPU:17, one launch (start us, length us, event | category | flops | bytes accessed | tf_op | source)
XLA Modules:
  0.0 106.8 jit_solution(2882962155635095557)
XLA Ops:
  0.0 0.7 convert_element_type.3
  0.7 0.8 copy.9
  1.5 0.7 reshape.17.pick_row
  2.1 0.7 reshape.20.pick_column
  2.8 0.5 fusion
  3.4 0.8 pad_maximum_fusion
  4.2 78.8 %exchange_and_band.1 = (bf16[8,256,1024]{2,1,0:T(8,128)(2,1)}, bf16[8,256,1024]{2,1,0:T(8,128)(2,1)}, f32[8,256,128]{2,1,0:T(8,128)}, bf16[16,2,2,128,128]{4,3,2,1,0:T(8,128)(2,1)}, s32[1,32]{1,0:T(1,128)}) custom-call(bf16[256,8192]{1,0:T(8,128)(2,1)} %queries.1, bf16[256,1024]{1,0:T(8,128)(2,1)} %keys.1, bf16[256,1024]{1,0:T(8,128)(2,1)} %values.1, ...), custom_call_target="tpu_custom_call" | custom-call | flops 4294967296 | bytes 12582912 | tf_op jit(solution)/shard_map/exchange_and_band/pallas_call | solution.py:318
  83.0 23.9 %picked_attention.1 = bf16[256,8192]{1,0:T(8,128)(2,1)} custom-call(s32[1,32]{1,0:T(1,128)} %get-tuple-element.10.slots, bf16[8,256,1024]{2,1,0:T(8,128)(2,1)} %get-tuple-element.11.rotated, bf16[8,256,1024]{2,1,0:T(8,128)(2,1)} %get-tuple-element.12.partial, f32[8,256,128]{2,1,0:T(8,128)} %get-tuple-element.13.stats, bf16[32,2,128,128]{3,2,1,0:T(8,128)(2,1)} %bitcast.1, ...), custom_call_target="tpu_custom_call" | custom-call | tf_op jit(solution)/shard_map/picked_attention/pallas_call | solution.py:368
  (1 shorter events, 0.0 us)

commit v2 on v1

--- a/solution.py
+++ b/solution.py
@@ -31,15 +31,10 @@
 
 
 def with_ones(v):
-    return jnp.concatenate([v, jnp.ones_like(v)], 1)
-
-
-def stack_heads(x):
-    return jnp.concatenate([x[:, n * HEAD_SIZE : (n + 1) * HEAD_SIZE] for n in range(GROUP)], 0)
-
-
-def head_rows(n):
-    return slice(n * BLOCK_TOKENS, (n + 1) * BLOCK_TOKENS)
+    return jnp.concatenate([v, jnp.ones((16, v.shape[1]), v.dtype)], 0)
+
+
+CHUNK = 4
 
 
 def flip(a, b, size):
@@ -51,11 +46,11 @@
 
 
 def exchange_kernel(
-    blocks, window, cap,
-    queries, keys, values, cosine, sine, pick_row, pick_column,
+    blocks, window, cap, relays,
+    queries, keys, values, cosine, sine, pick_row,
     rotated, partial, stats, landed, slots,
-    q_held, rotated_held, partial_held, stats_held, kv, near, far, answers, request, requests, scalars,
-    load_sem, store_sem, near_sem, far_sem, request_send, request_recv, scalar_sem, answer_send, answer_recv,
+    q_held, rotated_held, partial_held, stats_held, kv, near, far, relay_a, relay_b, answers, request, requests, scalars,
+    load_sem, store_sem, near_send, near_recv, far_send, far_recv, relay_send, relay_recv, forward_send, chip_send, request_send, request_recv, scalar_sem, answer_send, answer_recv,
 ):
     me = lax.axis_index("ctx")
     count = pick_row.shape[1]
@@ -78,11 +73,12 @@
 
     lax.fori_loop(0, KEY_VALUE_HEADS, start_load, 0)
 
-    row, column = pick_row[...], pick_column[...]
+    row = pick_row[...]
+    first = lax.broadcasted_iota(jnp.int32, (count, count), 0)
+    second = lax.broadcasted_iota(jnp.int32, (count, count), 1)
+    column = jnp.sum(jnp.where(first == second, row, 0), 1, keepdims=True)
     row_owner = jnp.maximum(row, 0) // blocks
     column_owner = jnp.maximum(column, 0) // blocks
-    first = lax.broadcasted_iota(jnp.int32, (count, count), 0)
-    second = lax.broadcasted_iota(jnp.int32, (count, count), 1)
     alike = (column_owner == row_owner) & (column >= 0) & (row >= 0)
     column_rank = jnp.sum((alike & (second < first)).astype(jnp.int32), 1, keepdims=True)
     row_rank = jnp.sum((alike & (first < second)).astype(jnp.int32), 0, keepdims=True)
@@ -98,7 +94,7 @@
         for head in range(KEY_VALUE_HEADS):
             columns = slice(head * HEAD_SIZE, (head + 1) * HEAD_SIZE)
             kv[i * KEY_VALUE_HEADS + head, 0] = rotate(keys[rows, columns], cosine[rows], sine[rows]).astype(jnp.bfloat16)
-            kv[i * KEY_VALUE_HEADS + head, 1] = values[rows, columns]
+            kv[i * KEY_VALUE_HEADS + head, 1] = values[rows, columns].astype(jnp.float32).T.astype(jnp.bfloat16)
 
     @pl.when(me < 1)
     def _():
@@ -128,23 +124,63 @@
 
     lax.fori_loop(0, me, start_ask, 0)
 
-    last = pl.ds((blocks - 1) * KEY_VALUE_HEADS, KEY_VALUE_HEADS)
-    send_near = pltpu.make_async_remote_copy(
-        src_ref=kv, dst_ref=near, send_sem=near_sem.at[0], recv_sem=near_sem.at[1],
-        device_id={"ctx": lax.rem(me + 1, window)},
-    )
-    send_far = pltpu.make_async_remote_copy(
-        src_ref=kv.at[last], dst_ref=far, send_sem=far_sem.at[0], recv_sem=far_sem.at[1],
-        device_id={"ctx": lax.rem(me + 2, window)},
-    )
-
-    @pl.when(me + 1 < window)
-    def _():
-        send_near.start()
-
-    @pl.when(me + 2 < window)
-    def _():
-        send_far.start()
+    def put(source, target, send_sem, recv_sem, to):
+        return pltpu.make_async_remote_copy(
+            src_ref=source, dst_ref=target, send_sem=send_sem, recv_sem=recv_sem,
+            device_id={"ctx": lax.rem(to + window, window)},
+        )
+
+    last = (blocks - 1) * KEY_VALUE_HEADS
+    near_part, far_part = blocks * KEY_VALUE_HEADS // 2, KEY_VALUE_HEADS // 2
+
+    def near_at(ref, half):
+        return ref.at[pl.ds(half * near_part, near_part)]
+
+    def far_at(ref, half, base=0):
+        return ref.at[pl.ds(base + half * far_part, far_part)]
+
+    def both(copies):
+        return [copies(half) for half in range(2)]
+
+    near_direct = both(lambda h: put(near_at(kv, h), near_at(near, h), near_send.at[h], near_recv.at[h], me + 1))
+    far_direct = both(lambda h: put(far_at(kv, h, last), far_at(far, h), far_send.at[h], far_recv.at[h], me + 2))
+    if relays:
+        core, x, z = me % 2, me // 2 % 2, me // 4
+        rows_z = window // 4
+        to_relay = [(me - 2, relay_a), (me + 4, relay_b)]
+        near_out = both(lambda h: put(near_at(kv, h), to_relay[h][1], relay_send.at[h], relay_recv.at[h], to_relay[h][0]))
+        far_out = both(
+            lambda h: put(
+                far_at(kv, h, last), far_at(to_relay[h][1], 0), relay_send.at[h], relay_recv.at[h], to_relay[h][0]
+            )
+        )
+        near_targets, far_targets = (me + 3, me - 3), (me + 4, me - 2)
+        relay_refs = (relay_a, relay_b)
+        near_on = both(
+            lambda h: put(relay_refs[h], near_at(near, h), forward_send.at[h], near_recv.at[h], near_targets[h])
+        )
+        far_on = both(
+            lambda h: put(far_at(relay_refs[h], 0), far_at(far, h), forward_send.at[h], far_recv.at[h], far_targets[h])
+        )
+        chip_far = both(lambda h: put(far_at(near, h, last), far_at(far, h), chip_send.at[h], far_recv.at[h], me + 1))
+        now = [
+            ((x == 1) & (core == 1) & (z < rows_z - 1), near_out),
+            ((x == 1) & (core == 0) & (z < rows_z - 1), far_out),
+            ((core == 1) & (x == 0), near_direct),
+            ((core == 0) & (x == 0), far_direct),
+            (core == 0, near_direct),
+        ]
+        as_relay = [((x == 0) & (z < rows_z - 1)), ((x == 1) & (z > 0))]
+        as_forwarder = (core == 0) & (me >= 2)
+    else:
+        now = [(me + 1 < window, near_direct), (me + 2 < window, far_direct)]
+
+    for condition, copies in now:
+
+        @pl.when(condition)
+        def _(copies=copies):
+            for copy in copies:
+                copy.start()
 
     def await_request(source, carry):
         asked(source).wait_recv()
@@ -174,19 +210,36 @@
 
     lax.fori_loop(0, window - 1, start_answer, 0)
 
+    if relays:
+        for half in range(2):
+            for at_core, arriving, on in ((1, near_out, near_on), (0, far_out, far_on)):
+
+                @pl.when(as_relay[half] & (core == at_core))
+                def _(half=half, arriving=arriving, on=on):
+                    arriving[half].wait_recv()
+                    on[half].start()
+
     @pl.when(me >= 1)
     def _():
-        send_near.wait_recv()
+        for copy in near_direct:
+            copy.wait_recv()
+
+    if relays:
+
+        @pl.when(as_forwarder)
+        def _():
+            for copy in chip_far:
+                copy.start()
 
     @pl.when(me >= 2)
     def _():
-        send_far.wait_recv()
+        for copy in far_direct:
+            copy.wait_recv()
 
     width = LOCAL_BAND_SIZE * BLOCK_TOKENS
     factor = HEAD_SIZE**-0.5 * log2_e
-    row = lax.broadcasted_iota(jnp.int32, (BLOCK_TOKENS, width), 0)
-    column = lax.broadcasted_iota(jnp.int32, (BLOCK_TOKENS, width), 1)
-    lane = lax.broadcasted_iota(jnp.int32, (BLOCK_TOKENS, 128), 1)
+    key = lax.broadcasted_iota(jnp.int32, (width, BLOCK_TOKENS), 0)
+    query = lax.broadcasted_iota(jnp.int32, (width, BLOCK_TOKENS), 1)
 
     def store(h):
         return [
@@ -200,28 +253,29 @@
         band = [far[h]] + [near[i * KEY_VALUE_HEADS + h] for i in range(blocks)]
         band = band + [kv[i * KEY_VALUE_HEADS + h] for i in range(blocks)]
         k_all = jnp.concatenate([b[0] for b in band], 0)
-        v_all = with_ones(jnp.concatenate([b[1] for b in band], 0))
+        v_all = with_ones(jnp.concatenate([b[1] for b in band], 1))
         for i in range(blocks):
             start = (me * blocks + i - (LOCAL_BAND_SIZE - 1)) * BLOCK_TOKENS
-            good = (column <= row + (LOCAL_BAND_SIZE - 1) * BLOCK_TOKENS) & (column + start >= 0)
-            bias = jnp.where(good, 0.0, masked_score)
+            good = (key <= query + (LOCAL_BAND_SIZE - 1) * BLOCK_TOKENS) & (key + start >= 0)
+            bias = jnp.concatenate([jnp.where(good, 0.0, masked_score)] * CHUNK, 1)
             rows = slice(i * BLOCK_TOKENS, (i + 1) * BLOCK_TOKENS)
             k = k_all[i * BLOCK_TOKENS : i * BLOCK_TOKENS + width]
-            v = v_all[i * BLOCK_TOKENS : i * BLOCK_TOKENS + width]
+            v = v_all[:, i * BLOCK_TOKENS : i * BLOCK_TOKENS + width]
             q_cosine, q_sine = cosine[rows] * factor, sine[rows] * factor
-            held = jnp.zeros((BLOCK_TOKENS, 128), jnp.float32)
-            for n in range(GROUP):
-                columns = slice(n * HEAD_SIZE, (n + 1) * HEAD_SIZE)
-                q = rotate(q_held[h, rows, columns], q_cosine, q_sine).astype(jnp.bfloat16)
-                rotated_held[h, rows, columns] = q
-                score = dot_nt(q, k) + bias
-                top = jnp.max(score, 1, keepdims=True)
+            for part in range(GROUP // CHUNK):
+                here = slice(part * CHUNK * BLOCK_TOKENS, (part + 1) * CHUNK * BLOCK_TOKENS)
+                heads = range(part * CHUNK, (part + 1) * CHUNK)
+                q = jnp.concatenate(
+                    [rotate(q_held[h, rows, n * HEAD_SIZE : (n + 1) * HEAD_SIZE], q_cosine, q_sine) for n in heads], 0
+                ).astype(jnp.bfloat16)
+                rotated_held[h, i, here] = q
+                score = dot_nt(k, q) + bias
+                top = jnp.max(score, 0, keepdims=True)
                 weight = jnp.exp2(score - top).astype(jnp.bfloat16)
-                summed = jnp.dot(weight, v, preferred_element_type=jnp.float32)
-                total = summed[:, HEAD_SIZE:]
-                partial_held[h, rows, columns] = (summed[:, :HEAD_SIZE] / total).astype(jnp.bfloat16)
-                held = jnp.where(lane == n, top + jnp.log2(total), held)
-            stats_held[h, rows] = held
+                summed = jnp.dot(v, weight, preferred_element_type=jnp.float32)
+                total = summed[HEAD_SIZE : HEAD_SIZE + 1]
+                partial_held[h, i, :, here] = (summed[:HEAD_SIZE] * (1.0 / total)).astype(jnp.bfloat16)
+                stats_held[h, i, :, here] = top + jnp.log2(total)
         for copy in store(h):
             copy.start()
         return carry
@@ -235,13 +289,25 @@
 
     lax.fori_loop(0, KEY_VALUE_HEADS, end_store, 0)
 
-    @pl.when(me + 1 < window)
-    def _():
-        send_near.wait_send()
-
-    @pl.when(me + 2 < window)
-    def _():
-        send_far.wait_send()
+    for condition, copies in now:
+
+        @pl.when(condition)
+        def _(copies=copies):
+            for copy in copies:
+                copy.wait_send()
+
+    if relays:
+        for half in range(2):
+            for at_core, on in ((1, near_on), (0, far_on)):
+
+                @pl.when(as_relay[half] & (core == at_core))
+                def _(half=half, on=on):
+                    on[half].wait_send()
+
+        @pl.when(as_forwarder)
+        def _():
+            for copy in chip_far:
+                copy.wait_send()
 
     def end_ask(owner, carry):
         ask(owner).wait_send()
@@ -265,31 +331,37 @@
 def pick_kernel(blocks, slots, rotated, partial, stats, *rest):
     landed, out = rest[:-1], rest[-1]
     head = pl.program_id(0)
-    column = lax.broadcasted_iota(jnp.int32, (1, PICKED_BLOCKS * BLOCK_TOKENS), 1)
     for i in range(blocks):
-        ks, vs = [], []
-        bias = jnp.zeros(column.shape, jnp.float32)
-        for p in range(PICKED_BLOCKS):
-            at = (i * KEY_VALUE_HEADS + head) * PICKED_BLOCKS + p
-            alive = slots[0, at] >= 0
-            pair = landed[i * PICKED_BLOCKS + p]
-            ks.append(jnp.where(alive, pair[0, 0], jnp.zeros_like(pair[0, 0])))
-            vs.append(jnp.where(alive, pair[0, 1], jnp.zeros_like(pair[0, 1])))
-            bias = jnp.where(column // BLOCK_TOKENS == p, jnp.where(alive, 0.0, masked_score), bias)
-        k = jnp.concatenate(ks, 0)
-        v = with_ones(jnp.concatenate(vs, 0))
+        alive = slots[0, (i * KEY_VALUE_HEADS + head) * PICKED_BLOCKS] >= 0
         rows = slice(i * BLOCK_TOKENS, (i + 1) * BLOCK_TOKENS)
-        score = dot_nt(stack_heads(rotated[0, rows]), k) + bias
-        near_top = jnp.concatenate([stats[0, rows, n : n + 1] for n in range(GROUP)], 0)
-        top = jnp.maximum(jnp.max(score, 1, keepdims=True), near_top)
-        weight = jnp.exp2(score - top).astype(jnp.bfloat16)
-        summed = jnp.dot(weight, v, preferred_element_type=jnp.float32)
-        near_weight = jnp.exp2(near_top - top)
-        held = stack_heads(partial[0, rows]).astype(jnp.float32)
-        result = (held * near_weight + summed[:, :HEAD_SIZE]) / (near_weight + summed[:, HEAD_SIZE:])
-        result = result.astype(jnp.bfloat16)
-        for n in range(GROUP):
-            out[rows, n * HEAD_SIZE : (n + 1) * HEAD_SIZE] = result[head_rows(n)]
+
+        def give(part, result):
+            for n in range(CHUNK):
+                at = (part * CHUNK + n) * HEAD_SIZE
+                out[rows, at : at + HEAD_SIZE] = result[:, n * BLOCK_TOKENS : (n + 1) * BLOCK_TOKENS].T.astype(jnp.bfloat16)
+
+        @pl.when(alive)
+        def _():
+            pair = landed[i * PICKED_BLOCKS : (i + 1) * PICKED_BLOCKS]
+            k = jnp.concatenate([p[0, 0] for p in pair], 0)
+            v = with_ones(jnp.concatenate([p[0, 1] for p in pair], 1))
+            for part in range(GROUP // CHUNK):
+                here = slice(part * CHUNK * BLOCK_TOKENS, (part + 1) * CHUNK * BLOCK_TOKENS)
+                score = dot_nt(k, rotated[0, i, here])
+                near_top = stats[0, i, :, here]
+                top = jnp.maximum(jnp.max(score, 0, keepdims=True), near_top)
+                weight = jnp.exp2(score - top).astype(jnp.bfloat16)
+                summed = jnp.dot(v, weight, preferred_element_type=jnp.float32)
+                near_weight = jnp.exp2(near_top - top)
+                inverse = 1.0 / (near_weight + summed[HEAD_SIZE : HEAD_SIZE + 1])
+                held = partial[0, i, :, here].astype(jnp.float32)
+                give(part, held * (near_weight * inverse) + summed[:HEAD_SIZE] * inverse)
+
+        @pl.when(jnp.logical_not(alive))
+        def _():
+            for part in range(GROUP // CHUNK):
+                here = slice(part * CHUNK * BLOCK_TOKENS, (part + 1) * CHUNK * BLOCK_TOKENS)
+                give(part, partial[0, i, :, here].astype(jnp.float32))
 
 
 def shards(queries, keys, values, positions, picks):
@@ -312,34 +384,45 @@
     here = pl.BlockSpec(memory_space=pltpu.VMEM)
     there = pl.BlockSpec(memory_space=pl.ANY)
     by_head = (KEY_VALUE_HEADS, tokens, per_head)
-    stats_dims = (KEY_VALUE_HEADS, tokens, 128)
+    stacked = GROUP * BLOCK_TOKENS
+    rotated_dims = (KEY_VALUE_HEADS, blocks, stacked, HEAD_SIZE)
+    partial_dims = (KEY_VALUE_HEADS, blocks, HEAD_SIZE, stacked)
+    stats_dims = (KEY_VALUE_HEADS, blocks, 1, stacked)
     width = LOCAL_BAND_SIZE * BLOCK_TOKENS
     limit = 56 * 1024 * 1024
     rotated, partial, stats, landed, slots = pl.pallas_call(
-        functools.partial(exchange_kernel, blocks, window, cap),
-        in_specs=[there] + [here] * 6,
+        functools.partial(exchange_kernel, blocks, window, cap, window == 16),
+        in_specs=[there] + [here] * 5,
         out_specs=[there] * 4 + [here],
         out_shape=[
-            jax.ShapeDtypeStruct(by_head, jnp.bfloat16),
-            jax.ShapeDtypeStruct(by_head, jnp.bfloat16),
+            jax.ShapeDtypeStruct(rotated_dims, jnp.bfloat16),
+            jax.ShapeDtypeStruct(partial_dims, jnp.bfloat16),
             jax.ShapeDtypeStruct(stats_dims, jnp.float32),
             jax.ShapeDtypeStruct((window, cap) + ENTRY, jnp.bfloat16),
             jax.ShapeDtypeStruct((1, count), jnp.int32),
         ],
         scratch_shapes=[
             pltpu.VMEM(by_head, jnp.bfloat16),
-            pltpu.VMEM(by_head, jnp.bfloat16),
-            pltpu.VMEM(by_head, jnp.bfloat16),
+            pltpu.VMEM(rotated_dims, jnp.bfloat16),
+            pltpu.VMEM(partial_dims, jnp.bfloat16),
             pltpu.VMEM(stats_dims, jnp.float32),
             pltpu.VMEM((entries,) + ENTRY, jnp.bfloat16),
             pltpu.VMEM((entries,) + ENTRY, jnp.bfloat16),
             pltpu.VMEM((KEY_VALUE_HEADS,) + ENTRY, jnp.bfloat16),
+            pltpu.VMEM((entries // 2,) + ENTRY, jnp.bfloat16),
+            pltpu.VMEM((entries // 2,) + ENTRY, jnp.bfloat16),
             pltpu.VMEM((window, cap) + ENTRY, jnp.bfloat16),
             pltpu.VMEM((1, lanes), jnp.int32),
             pltpu.VMEM((window, 1, lanes), jnp.int32),
             pltpu.SMEM((window, 1, lanes), jnp.int32),
             pltpu.SemaphoreType.DMA((KEY_VALUE_HEADS,)),
             pltpu.SemaphoreType.DMA((3, KEY_VALUE_HEADS)),
+            pltpu.SemaphoreType.DMA((2,)),
+            pltpu.SemaphoreType.DMA((2,)),
+            pltpu.SemaphoreType.DMA((2,)),
+            pltpu.SemaphoreType.DMA((2,)),
+            pltpu.SemaphoreType.DMA((2,)),
+            pltpu.SemaphoreType.DMA((2,)),
             pltpu.SemaphoreType.DMA((2,)),
             pltpu.SemaphoreType.DMA((2,)),
             pltpu.SemaphoreType.DMA((window,)),
@@ -355,7 +438,7 @@
             transcendentals=tokens * QUERY_HEADS * width,
         ),
         name="exchange_and_band",
-    )(queries, keys, values, cosine, sine, picks.reshape(1, count), picks.reshape(count, 1))
+    )(queries, keys, values, cosine, sine, picks.reshape(1, count))
 
     def slot_spec(i, p):
         def place(h, slot):
@@ -363,14 +446,16 @@
 
         return pl.BlockSpec((1,) + ENTRY, place)
 
-    by_head_spec = pl.BlockSpec((1, tokens, per_head), lambda h, *_: (h, 0, 0))
+    def head_spec(dims):
+        return pl.BlockSpec((1,) + dims[1:], lambda h, *_: (h, 0, 0, 0))
+
     landed = landed.reshape((window * cap,) + ENTRY)
     return pl.pallas_call(
         functools.partial(pick_kernel, blocks),
         grid_spec=pltpu.PrefetchScalarGridSpec(
             num_scalar_prefetch=1,
             grid=(KEY_VALUE_HEADS,),
-            in_specs=[by_head_spec, by_head_spec, pl.BlockSpec((1, tokens, 128), lambda h, *_: (h, 0, 0))]
+            in_specs=[head_spec(rotated_dims), head_spec(partial_dims), head_spec(stats_dims)]
             + [slot_spec(i, p) for i in range(blocks) for p in range(PICKED_BLOCKS)],
             out_specs=pl.BlockSpec((tokens, per_head), lambda h, *_: (0, h)),
         ),

time: 107 us -> 102 us (0.953)
  Pallas kernels: 103 us -> 98.5 us
    pallas_call x1, Pallas kernels: 23.9 us -> 13.5 us  [shards(): pl.pallas_call(functools.partial(pick_kernel, blocks), grid_spec=pltpu.Pr...]
    pallas_call x1, Pallas kernels: 78.8 us -> 85 us  [shards(): pl.pallas_call(functools.partial(exchange_kernel, blocks, window, cap, wi...]
where the time goes in v2:
time: 102 us
  Pallas kernels  98.5 us (97%)
  other arithmetic  2.08 us (2%)
  local copies, waits for them, and re-layouts  1.38 us (1%)
    pallas_call x1, Pallas kernels, shards(): pl.pallas_call(functools.partial(exchange_kernel, blocks, window, cap, wi...  85 us
    pallas_call x1, Pallas kernels, shards(): pl.pallas_call(functools.partial(pick_kernel, blocks), grid_spec=pltpu.Pr...  13.5 us

profile of v2, /device:TPU:17, one launch (start us, length us, event | category | flops | bytes accessed | tf_op | source)
XLA Modules:
  0.0 102.0 jit_solution(17911378534967951148)
XLA Ops:
  0.0 0.7 convert_element_type.3
  0.7 0.8 copy.7
  1.5 0.6 reshape.14.pick_row
  2.1 0.5 fusion
  2.6 0.9 pad_maximum_fusion
  3.5 85.0 %exchange_and_band.1 = (bf16[8,2,1024,128]{3,2,1,0:T(8,128)(2,1)}, bf16[8,2,128,1024]{3,2,1,0:T(8,128)(2,1)}, f32[8,2,1,1024]{3,2,1,0:T(1,128)}, bf16[16,2,2,128,128]{4,3,2,1,0:T(8,128)(2,1)}, s32[1,32]{1,0:T(1,128)}) custom-call(bf16[256,8192]{1,0:T(8,128)(2,1)} %queries.1, bf16[256,1024]{1,0:T(8,128)(2,1)} %keys.1, bf16[256,1024]{1,0:T(8,128)(2,1)} %values.1, ...), custom_call_target="tpu_custom_call" | custom-call | flops 4294967296 | bytes 12582912 | tf_op jit(solution)/shard_map/exchange_and_band/pallas_call | solution.py:393
  88.4 13.5 %picked_attention.1 = bf16[256,8192]{1,0:T(8,128)(2,1)} custom-call(s32[1,32]{1,0:T(1,128)} %get-tuple-element.10.slots, bf16[8,2,1024,128]{3,2,1,0:T(8,128)(2,1)} %get-tuple-element.11.rotated, bf16[8,2,128,1024]{3,2,1,0:T(8,128)(2,1)} %get-tuple-element.12.partial, f32[8,2,1,1024]{3,2,1,0:T(1,128)} %get-tuple-element.13.stats, ...), custom_call_target="tpu_custom_call" | custom-call | tf_op jit(solution)/shard_map/picked_attention/pallas_call | solution.py:453
  (1 shorter events, 0.0 us)

commit v3 on v2

--- a/solution.py
+++ b/solution.py
@@ -48,9 +48,9 @@
 def exchange_kernel(
     blocks, window, cap, relays,
     queries, keys, values, cosine, sine, pick_row,
-    rotated, partial, stats, landed, slots,
-    q_held, rotated_held, partial_held, stats_held, kv, near, far, relay_a, relay_b, answers, request, requests, scalars,
-    load_sem, store_sem, near_send, near_recv, far_send, far_recv, relay_send, relay_recv, forward_send, chip_send, request_send, request_recv, scalar_sem, answer_send, answer_recv,
+    partial, stats, slot_partial, slot_stats, slots,
+    q_held, rotated, partial_held, stats_held, slot_partial_held, slot_stats_held, landed, kv, near, far, relay_a, relay_b, answers, request, requests, scalars, users, user_scalars,
+    load_sem, store_sem, near_send, near_recv, far_send, far_recv, relay_send, relay_recv, forward_send, chip_send, request_send, request_recv, scalar_sem, slot_sem, answer_send, answer_recv,
 ):
     me = lax.axis_index("ctx")
     count = pick_row.shape[1]
@@ -88,6 +88,7 @@
     lane = lax.broadcasted_iota(jnp.int32, (count, request.shape[1]), 1)
     hit = (column_owner * cap + column_rank == lane) & (column >= 0)
     request[...] = jnp.sum(jnp.where(hit, entry, 0), 0, keepdims=True)
+    users[...] = jnp.sum(jnp.where(hit, order // PICKED_BLOCKS, 0), 0, keepdims=True)
 
     for i in range(blocks):
         rows = slice(i * BLOCK_TOKENS, (i + 1) * BLOCK_TOKENS)
@@ -162,16 +163,15 @@
         far_on = both(
             lambda h: put(far_at(relay_refs[h], 0), far_at(far, h), forward_send.at[h], far_recv.at[h], far_targets[h])
         )
-        chip_far = both(lambda h: put(far_at(near, h, last), far_at(far, h), chip_send.at[h], far_recv.at[h], me + 1))
+        beside_far = both(lambda h: put(far_at(relay_b, h), far_at(far, h), chip_send.at[h], far_recv.at[h], me - 2))
         now = [
             ((x == 1) & (core == 1) & (z < rows_z - 1), near_out),
             ((x == 1) & (core == 0) & (z < rows_z - 1), far_out),
             ((core == 1) & (x == 0), near_direct),
-            ((core == 0) & (x == 0), far_direct),
+            (x == 0, far_direct),
             (core == 0, near_direct),
         ]
         as_relay = [((x == 0) & (z < rows_z - 1)), ((x == 1) & (z > 0))]
-        as_forwarder = (core == 0) & (me >= 2)
     else:
         now = [(me + 1 < window, near_direct), (me + 2 < window, far_direct)]
 
@@ -208,29 +208,32 @@
 
         return carry
 
-    lax.fori_loop(0, window - 1, start_answer, 0)
+    ahead = 2 if relays else window - 1
+    lax.fori_loop(0, ahead, start_answer, 0)
 
     if relays:
         for half in range(2):
             for at_core, arriving, on in ((1, near_out, near_on), (0, far_out, far_on)):
 
                 @pl.when(as_relay[half] & (core == at_core))
-                def _(half=half, arriving=arriving, on=on):
+                def _(half=half, at_core=at_core, arriving=arriving, on=on):
                     arriving[half].wait_recv()
                     on[half].start()
+                    if half == 1 and at_core == 1:
+                        for copy in beside_far:
+                            copy.start()
+
+        lax.fori_loop(ahead, window - 1, start_answer, 0)
+
+    to_users = pltpu.make_async_copy(users, user_scalars, scalar_sem)
+    to_users.start()
+    to_users.wait()
 
     @pl.when(me >= 1)
     def _():
         for copy in near_direct:
             copy.wait_recv()
 
-    if relays:
-
-        @pl.when(as_forwarder)
-        def _():
-            for copy in chip_far:
-                copy.start()
-
     @pl.when(me >= 2)
     def _():
         for copy in far_direct:
@@ -243,9 +246,8 @@
 
     def store(h):
         return [
-            pltpu.make_async_copy(rotated_held.at[h], rotated.at[h], store_sem.at[0, h]),
-            pltpu.make_async_copy(partial_held.at[h], partial.at[h], store_sem.at[1, h]),
-            pltpu.make_async_copy(stats_held.at[h], stats.at[h], store_sem.at[2, h]),
+            pltpu.make_async_copy(partial_held.at[h], partial.at[h], store_sem.at[0, h]),
+            pltpu.make_async_copy(stats_held.at[h], stats.at[h], store_sem.at[1, h]),
         ]
 
     def one_head(h, carry):
@@ -268,7 +270,7 @@
                 q = jnp.concatenate(
                     [rotate(q_held[h, rows, n * HEAD_SIZE : (n + 1) * HEAD_SIZE], q_cosine, q_sine) for n in heads], 0
                 ).astype(jnp.bfloat16)
-                rotated_held[h, i, here] = q
+                rotated[i * KEY_VALUE_HEADS + h, here] = q
                 score = dot_nt(k, q) + bias
                 top = jnp.max(score, 0, keepdims=True)
                 weight = jnp.exp2(score - top).astype(jnp.bfloat16)
@@ -282,6 +284,46 @@
 
     lax.fori_loop(0, KEY_VALUE_HEADS, one_head, 0)
 
+    def store_slots(source, side):
+        place = pl.ds(source * cap, cap)
+        return [
+            pltpu.make_async_copy(slot_partial_held.at[side], slot_partial.at[place], slot_sem.at[0, side]),
+            pltpu.make_async_copy(slot_stats_held.at[side], slot_stats.at[place], slot_sem.at[1, side]),
+        ]
+
+    def one_source(source, carry):
+        side = source % 2
+        answer(source, source, source).wait_recv()
+
+        @pl.when(source >= 2)
+        def _():
+            for copy in store_slots(source - 2, side):
+                copy.wait()
+
+        for c in range(cap):
+            k = landed[source, c, 0]
+            v = with_ones(landed[source, c, 1])
+            q = rotated[user_scalars[0, source * cap + c]]
+            score = dot_nt(k, q)
+            top = jnp.max(score, 0, keepdims=True)
+            weight = jnp.exp2(score - top).astype(jnp.bfloat16)
+            summed = jnp.dot(v, weight, preferred_element_type=jnp.float32)
+            total = summed[HEAD_SIZE : HEAD_SIZE + 1]
+            slot_partial_held[side, c] = (summed[:HEAD_SIZE] * (1.0 / total)).astype(jnp.bfloat16)
+            slot_stats_held[side, c] = top + jnp.log2(total)
+        for copy in store_slots(source, side):
+            copy.start()
+        return carry
+
+    lax.fori_loop(0, me, one_source, 0)
+
+    def end_slots(source, carry):
+        for copy in store_slots(source, source % 2):
+            copy.wait()
+        return carry
+
+    lax.fori_loop(jnp.maximum(me - 2, 0), me, end_slots, 0)
+
     def end_store(h, carry):
         for copy in store(h):
             copy.wait()
@@ -304,9 +346,9 @@
                 def _(half=half, on=on):
                     on[half].wait_send()
 
-        @pl.when(as_forwarder)
+        @pl.when(as_relay[1] & (core == 1))
         def _():
-            for copy in chip_far:
+            for copy in beside_far:
                 copy.wait_send()
 
     def end_ask(owner, carry):
@@ -321,19 +363,15 @@
 
     lax.fori_loop(me + 1, window, end_answer, 0)
 
-    def arrive(source, carry):
-        answer(source, source, source).wait_recv()
-        return carry
-
-    lax.fori_loop(0, me, arrive, 0)
-
-
-def pick_kernel(blocks, slots, rotated, partial, stats, *rest):
-    landed, out = rest[:-1], rest[-1]
+
+def merge_kernel(blocks, slots, partial, stats, *rest):
+    slot_count = blocks * PICKED_BLOCKS
+    slot_partials, slot_stats, out = rest[:slot_count], rest[slot_count:-1], rest[-1]
     head = pl.program_id(0)
     for i in range(blocks):
         alive = slots[0, (i * KEY_VALUE_HEADS + head) * PICKED_BLOCKS] >= 0
         rows = slice(i * BLOCK_TOKENS, (i + 1) * BLOCK_TOKENS)
+        pair = range(i * PICKED_BLOCKS, (i + 1) * PICKED_BLOCKS)
 
         def give(part, result):
             for n in range(CHUNK):
@@ -342,20 +380,14 @@
 
         @pl.when(alive)
         def _():
-            pair = landed[i * PICKED_BLOCKS : (i + 1) * PICKED_BLOCKS]
-            k = jnp.concatenate([p[0, 0] for p in pair], 0)
-            v = with_ones(jnp.concatenate([p[0, 1] for p in pair], 1))
             for part in range(GROUP // CHUNK):
                 here = slice(part * CHUNK * BLOCK_TOKENS, (part + 1) * CHUNK * BLOCK_TOKENS)
-                score = dot_nt(k, rotated[0, i, here])
-                near_top = stats[0, i, :, here]
-                top = jnp.maximum(jnp.max(score, 0, keepdims=True), near_top)
-                weight = jnp.exp2(score - top).astype(jnp.bfloat16)
-                summed = jnp.dot(v, weight, preferred_element_type=jnp.float32)
-                near_weight = jnp.exp2(near_top - top)
-                inverse = 1.0 / (near_weight + summed[HEAD_SIZE : HEAD_SIZE + 1])
-                held = partial[0, i, :, here].astype(jnp.float32)
-                give(part, held * (near_weight * inverse) + summed[:HEAD_SIZE] * inverse)
+                logs = [stats[0, i, :, here]] + [slot_stats[p][0, :, here] for p in pair]
+                terms = [partial[0, i, :, here]] + [slot_partials[p][0, :, here] for p in pair]
+                top = functools.reduce(jnp.maximum, logs)
+                weights = [jnp.exp2(log - top) for log in logs]
+                inverse = 1.0 / sum(weights)
+                give(part, sum(t.astype(jnp.float32) * (w * inverse) for t, w in zip(terms, weights)))
 
         @pl.when(jnp.logical_not(alive))
         def _():
@@ -385,27 +417,30 @@
     there = pl.BlockSpec(memory_space=pl.ANY)
     by_head = (KEY_VALUE_HEADS, tokens, per_head)
     stacked = GROUP * BLOCK_TOKENS
-    rotated_dims = (KEY_VALUE_HEADS, blocks, stacked, HEAD_SIZE)
+    slot_count = window * cap
     partial_dims = (KEY_VALUE_HEADS, blocks, HEAD_SIZE, stacked)
     stats_dims = (KEY_VALUE_HEADS, blocks, 1, stacked)
     width = LOCAL_BAND_SIZE * BLOCK_TOKENS
     limit = 56 * 1024 * 1024
-    rotated, partial, stats, landed, slots = pl.pallas_call(
+    partial, stats, slot_partial, slot_stats, slots = pl.pallas_call(
         functools.partial(exchange_kernel, blocks, window, cap, window == 16),
         in_specs=[there] + [here] * 5,
         out_specs=[there] * 4 + [here],
         out_shape=[
-            jax.ShapeDtypeStruct(rotated_dims, jnp.bfloat16),
             jax.ShapeDtypeStruct(partial_dims, jnp.bfloat16),
             jax.ShapeDtypeStruct(stats_dims, jnp.float32),
-            jax.ShapeDtypeStruct((window, cap) + ENTRY, jnp.bfloat16),
+            jax.ShapeDtypeStruct((slot_count, HEAD_SIZE, stacked), jnp.bfloat16),
+            jax.ShapeDtypeStruct((slot_count, 1, stacked), jnp.float32),
             jax.ShapeDtypeStruct((1, count), jnp.int32),
         ],
         scratch_shapes=[
             pltpu.VMEM(by_head, jnp.bfloat16),
-            pltpu.VMEM(rotated_dims, jnp.bfloat16),
+            pltpu.VMEM((entries, stacked, HEAD_SIZE), jnp.bfloat16),
             pltpu.VMEM(partial_dims, jnp.bfloat16),
             pltpu.VMEM(stats_dims, jnp.float32),
+            pltpu.VMEM((2, cap, HEAD_SIZE, stacked), jnp.bfloat16),
+            pltpu.VMEM((2, cap, 1, stacked), jnp.float32),
+            pltpu.VMEM((window, cap) + ENTRY, jnp.bfloat16),
             pltpu.VMEM((entries,) + ENTRY, jnp.bfloat16),
             pltpu.VMEM((entries,) + ENTRY, jnp.bfloat16),
             pltpu.VMEM((KEY_VALUE_HEADS,) + ENTRY, jnp.bfloat16),
@@ -415,8 +450,10 @@
             pltpu.VMEM((1, lanes), jnp.int32),
             pltpu.VMEM((window, 1, lanes), jnp.int32),
             pltpu.SMEM((window, 1, lanes), jnp.int32),
+            pltpu.VMEM((1, lanes), jnp.int32),
+            pltpu.SMEM((1, lanes), jnp.int32),
             pltpu.SemaphoreType.DMA((KEY_VALUE_HEADS,)),
-            pltpu.SemaphoreType.DMA((3, KEY_VALUE_HEADS)),
+            pltpu.SemaphoreType.DMA((2, KEY_VALUE_HEADS)),
             pltpu.SemaphoreType.DMA((2,)),
             pltpu.SemaphoreType.DMA((2,)),
             pltpu.SemaphoreType.DMA((2,)),
@@ -428,6 +465,7 @@
             pltpu.SemaphoreType.DMA((window,)),
             pltpu.SemaphoreType.DMA((window,)),
             pltpu.SemaphoreType.DMA,
+            pltpu.SemaphoreType.DMA((2, 2)),
             pltpu.SemaphoreType.DMA((window,)),
             pltpu.SemaphoreType.DMA((window,)),
         ],
@@ -440,29 +478,34 @@
         name="exchange_and_band",
     )(queries, keys, values, cosine, sine, picks.reshape(1, count))
 
-    def slot_spec(i, p):
-        def place(h, slot):
-            return (jnp.maximum(slot[0, (i * KEY_VALUE_HEADS + h) * PICKED_BLOCKS + p], 0), 0, 0, 0)
-
-        return pl.BlockSpec((1,) + ENTRY, place)
+    def slot_specs(dims):
+        def spec(at):
+            def place(h, slot):
+                i, p = at // PICKED_BLOCKS, at % PICKED_BLOCKS
+                return (jnp.maximum(slot[0, (i * KEY_VALUE_HEADS + h) * PICKED_BLOCKS + p], 0), 0, 0)
+
+            return pl.BlockSpec((1,) + dims, place)
+
+        return [spec(at) for at in range(blocks * PICKED_BLOCKS)]
 
     def head_spec(dims):
         return pl.BlockSpec((1,) + dims[1:], lambda h, *_: (h, 0, 0, 0))
 
-    landed = landed.reshape((window * cap,) + ENTRY)
+    copies = blocks * PICKED_BLOCKS
     return pl.pallas_call(
-        functools.partial(pick_kernel, blocks),
+        functools.partial(merge_kernel, blocks),
         grid_spec=pltpu.PrefetchScalarGridSpec(
             num_scalar_prefetch=1,
             grid=(KEY_VALUE_HEADS,),
-            in_specs=[head_spec(rotated_dims), head_spec(partial_dims), head_spec(stats_dims)]
-            + [slot_spec(i, p) for i in range(blocks) for p in range(PICKED_BLOCKS)],
+            in_specs=[head_spec(partial_dims), head_spec(stats_dims)]
+            + slot_specs((HEAD_SIZE, stacked))
+            + slot_specs((1, stacked)),
             out_specs=pl.BlockSpec((tokens, per_head), lambda h, *_: (0, h)),
         ),
         out_shape=jax.ShapeDtypeStruct(queries.shape, jnp.bfloat16),
         compiler_params=pltpu.CompilerParams(vmem_limit_bytes=limit),
-        name="picked_attention",
-    )(slots, rotated, partial, stats, *[landed] * (blocks * PICKED_BLOCKS))
+        name="merge",
+    )(slots, partial, stats, *[slot_partial] * copies, *[slot_stats] * copies)
 
 
 def solution(mesh):

time: 102 us -> 94.7 us (0.928)
  Pallas kernels: 98.5 us -> 90.9 us
    pallas_call x1, Pallas kernels: 13.5 us -> 9.71 us  [shards(): pl.pallas_call(functools.partial(merge_kernel, blocks), grid_spec=pltpu.P...]
    pallas_call x1, Pallas kernels: 85 us -> 81.2 us  [shards(): pl.pallas_call(functools.partial(exchange_kernel, blocks, window, cap, wi...]
where the time goes in v3:
time: 94.7 us; the launch traced here: 94.4 us
  Pallas kernels  90.9 us (96%)
  other arithmetic  2.07 us (2%)
  local copies, waits for them, and re-layouts  1.39 us (1%)
    pallas_call x1, Pallas kernels, shards(): pl.pallas_call(functools.partial(exchange_kernel, blocks, window, cap, wi...  81.2 us
    pallas_call x1, Pallas kernels, shards(): pl.pallas_call(functools.partial(merge_kernel, blocks), grid_spec=pltpu.P...  9.71 us

profile of v3, /device:TPU:17, one launch (start us, length us, event | category | flops | bytes accessed | tf_op | source)
XLA Modules:
  0.0 94.4 jit_solution(3082970118514110949)
XLA Ops:
  0.0 0.7 convert_element_type.3
  0.7 0.8 copy.7
  1.5 0.6 reshape.11.pick_row
  2.1 0.5 fusion
  2.6 0.8 pad_maximum_fusion
  3.5 81.2 %exchange_and_band.1 = (bf16[8,2,128,1024]{3,2,1,0:T(8,128)(2,1)}, f32[8,2,1,1024]{3,2,1,0:T(1,128)}, bf16[32,128,1024]{2,1,0:T(8,128)(2,1)}, f32[32,1,1024]{2,1,0:T(1,128)}, s32[1,32]{1,0:T(1,128)}) custom-call(bf16[256,8192]{1,0:T(8,128)(2,1)} %queries.1, bf16[256,1024]{1,0:T(8,128)(2,1)} %keys.1, bf16[256,1024]{1,0:T(8,128)(2,1)} %values.1, ...), custom_call_target="tpu_custom_call" | custom-call | flops 4294967296 | bytes 12582912 | tf_op jit(solution)/shard_map/exchange_and_band/pallas_call | solution.py:425
  84.7 9.7 %merge.1 = bf16[256,8192]{1,0:T(8,128)(2,1)} custom-call(s32[1,32]{1,0:T(1,128)} %get-tuple-element.10.slots, bf16[8,2,128,1024]{3,2,1,0:T(8,128)(2,1)} %get-tuple-element.11.partial, f32[8,2,1,1024]{3,2,1,0:T(1,128)} %get-tuple-element.12.stats, bf16[32,128,1024]{2,1,0:T(8,128)(2,1)} %get-tuple-element.13.rest_0_.rest_1_.rest_2_.rest_3_, ...), custom_call_target="tpu_custom_call" | custom-call | tf_op jit(solution)/shard_map/merge/pallas_call | solution.py:495
  (1 shorter events, 0.0 us)

commit v4 on v3

--- a/solution.py
+++ b/solution.py
@@ -197,19 +197,21 @@
             device_id={"ctx": other},
         )
 
+    def gather_answer(other, carry):
+        for c in range(cap):
+            answers[other, c] = kv[scalars[other, 0, me * cap + c]]
+        return carry
+
+    lax.fori_loop(me + 1, window, gather_answer, 0)
+
     def start_answer(j, carry):
         other = flip(me, window - 1 - j, window)
 
         @pl.when(other > me)
         def _():
-            for c in range(cap):
-                answers[other, c] = kv[scalars[other, 0, me * cap + c]]
             answer(other, other, me).start()
 
         return carry
-
-    ahead = 2 if relays else window - 1
-    lax.fori_loop(0, ahead, start_answer, 0)
 
     if relays:
         for half in range(2):
@@ -223,7 +225,7 @@
                         for copy in beside_far:
                             copy.start()
 
-        lax.fori_loop(ahead, window - 1, start_answer, 0)
+    lax.fori_loop(0, window - 1, start_answer, 0)
 
     to_users = pltpu.make_async_copy(users, user_scalars, scalar_sem)
     to_users.start()
@@ -291,31 +293,36 @@
             pltpu.make_async_copy(slot_stats_held.at[side], slot_stats.at[place], slot_sem.at[1, side]),
         ]
 
-    def one_source(source, carry):
-        side = source % 2
-        answer(source, source, source).wait_recv()
-
-        @pl.when(source >= 2)
+    def one_source(j, done):
+        source = flip(me, window - 1 - j, window)
+        side = done % 2
+
+        @pl.when(source < me)
         def _():
-            for copy in store_slots(source - 2, side):
-                copy.wait()
-
-        for c in range(cap):
-            k = landed[source, c, 0]
-            v = with_ones(landed[source, c, 1])
-            q = rotated[user_scalars[0, source * cap + c]]
-            score = dot_nt(k, q)
-            top = jnp.max(score, 0, keepdims=True)
-            weight = jnp.exp2(score - top).astype(jnp.bfloat16)
-            summed = jnp.dot(v, weight, preferred_element_type=jnp.float32)
-            total = summed[HEAD_SIZE : HEAD_SIZE + 1]
-            slot_partial_held[side, c] = (summed[:HEAD_SIZE] * (1.0 / total)).astype(jnp.bfloat16)
-            slot_stats_held[side, c] = top + jnp.log2(total)
-        for copy in store_slots(source, side):
-            copy.start()
-        return carry
-
-    lax.fori_loop(0, me, one_source, 0)
+            answer(source, source, source).wait_recv()
+
+            @pl.when(done >= 2)
+            def _():
+                for copy in store_slots(source, side):
+                    copy.wait()
+
+            for c in range(cap):
+                k = landed[source, c, 0]
+                v = with_ones(landed[source, c, 1])
+                q = rotated[user_scalars[0, source * cap + c]]
+                score = dot_nt(k, q)
+                top = jnp.max(score, 0, keepdims=True)
+                weight = jnp.exp2(score - top).astype(jnp.bfloat16)
+                summed = jnp.dot(v, weight, preferred_element_type=jnp.float32)
+                total = summed[HEAD_SIZE : HEAD_SIZE + 1]
+                slot_partial_held[side, c] = (summed[:HEAD_SIZE] * (1.0 / total)).astype(jnp.bfloat16)
+                slot_stats_held[side, c] = top + jnp.log2(total)
+            for copy in store_slots(source, side):
+                copy.start()
+
+        return done + jnp.where(source < me, 1, 0)
+
+    lax.fori_loop(0, window - 1, one_source, jnp.int32(0))
 
     def end_slots(source, carry):
         for copy in store_slots(source, source % 2):
@@ -368,6 +375,9 @@
     slot_count = blocks * PICKED_BLOCKS
     slot_partials, slot_stats, out = rest[:slot_count], rest[slot_count:-1], rest[-1]
     head = pl.program_id(0)
+    row = lax.broadcasted_iota(jnp.int32, (BLOCK_TOKENS, BLOCK_TOKENS), 0)
+    column = lax.broadcasted_iota(jnp.int32, (BLOCK_TOKENS, BLOCK_TOKENS), 1)
+    identity = jnp.where(row == column, 1.0, 0.0).astype(jnp.bfloat16)
     for i in range(blocks):
         alive = slots[0, (i * KEY_VALUE_HEADS + head) * PICKED_BLOCKS] >= 0
         rows = slice(i * BLOCK_TOKENS, (i + 1) * BLOCK_TOKENS)
@@ -376,7 +386,8 @@
         def give(part, result):
             for n in range(CHUNK):
                 at = (part * CHUNK + n) * HEAD_SIZE
-                out[rows, at : at + HEAD_SIZE] = result[:, n * BLOCK_TOKENS : (n + 1) * BLOCK_TOKENS].T.astype(jnp.bfloat16)
+                turned = dot_nt(identity, result[:, n * BLOCK_TOKENS : (n + 1) * BLOCK_TOKENS].astype(jnp.bfloat16))
+                out[rows, at : at + HEAD_SIZE] = turned.astype(jnp.bfloat16)
 
         @pl.when(alive)
         def _():

time: 94.7 us -> 91.3 us (0.964)
  the two profiles are of different devices: /device:TPU:17 before, /device:TPU:27 now
where the time goes in v4:
time: 91.3 us; the launch traced here: 90.9 us
  Pallas kernels  87.4 us (96%)
  other arithmetic  2.07 us (2%)
  local copies, waits for them, and re-layouts  1.39 us (2%)
    pallas_call x1, Pallas kernels, shards(): pl.pallas_call(functools.partial(exchange_kernel, blocks, window, cap, wi...  75.6 us
    pallas_call x1, Pallas kernels, shards(): pl.pallas_call(functools.partial(merge_kernel, blocks), grid_spec=pltpu.P...  11.8 us

profile of v4, /device:TPU:27, one launch (start us, length us, event | category | flops | bytes accessed | tf_op | source)
XLA Modules:
  0.0 90.9 jit_solution(3878190930628612824)
XLA Ops:
  0.0 0.7 convert_element_type.3
  0.7 0.8 copy.7
  1.5 0.6 reshape.11.pick_row
  2.1 0.5 fusion
  2.6 0.8 pad_maximum_fusion
  3.5 75.6 %exchange_and_band.1 = (bf16[8,2,128,1024]{3,2,1,0:T(8,128)(2,1)}, f32[8,2,1,1024]{3,2,1,0:T(1,128)}, bf16[32,128,1024]{2,1,0:T(8,128)(2,1)}, f32[32,1,1024]{2,1,0:T(1,128)}, s32[1,32]{1,0:T(1,128)}) custom-call(bf16[256,8192]{1,0:T(8,128)(2,1)} %queries.1, bf16[256,1024]{1,0:T(8,128)(2,1)} %keys.1, bf16[256,1024]{1,0:T(8,128)(2,1)} %values.1, ...), custom_call_target="tpu_custom_call" | custom-call | flops 4294967296 | bytes 12582912 | tf_op jit(solution)/shard_map/exchange_and_band/pallas_call | solution.py:436
  79.1 11.8 %merge.1 = bf16[256,8192]{1,0:T(8,128)(2,1)} custom-call(s32[1,32]{1,0:T(1,128)} %get-tuple-element.10.slots, bf16[8,2,128,1024]{3,2,1,0:T(8,128)(2,1)} %get-tuple-element.11.partial, f32[8,2,1,1024]{3,2,1,0:T(1,128)} %get-tuple-element.12.stats, bf16[32,128,1024]{2,1,0:T(8,128)(2,1)} %get-tuple-element.13.rest_0_.rest_1_.rest_2_.rest_3_, ...), custom_call_target="tpu_custom_call" | custom-call | tf_op jit(solution)/shard_map/merge/pallas_call | solution.py:506
  (1 shorter events, 0.0 us)

commit v5 on v4

--- a/solution.py
+++ b/solution.py
@@ -168,7 +168,7 @@
             ((x == 1) & (core == 1) & (z < rows_z - 1), near_out),
             ((x == 1) & (core == 0) & (z < rows_z - 1), far_out),
             ((core == 1) & (x == 0), near_direct),
-            (x == 0, far_direct),
+            ((core == 0) & (x == 0), far_direct),
             (core == 0, near_direct),
         ]
         as_relay = [((x == 0) & (z < rows_z - 1)), ((x == 1) & (z > 0))]
@@ -197,21 +197,19 @@
             device_id={"ctx": other},
         )
 
-    def gather_answer(other, carry):
-        for c in range(cap):
-            answers[other, c] = kv[scalars[other, 0, me * cap + c]]
-        return carry
-
-    lax.fori_loop(me + 1, window, gather_answer, 0)
-
     def start_answer(j, carry):
         other = flip(me, window - 1 - j, window)
 
         @pl.when(other > me)
         def _():
+            for c in range(cap):
+                answers[other, c] = kv[scalars[other, 0, me * cap + c]]
             answer(other, other, me).start()
 
         return carry
+
+    ahead = 2
+    lax.fori_loop(0, ahead, start_answer, 0)
 
     if relays:
         for half in range(2):
@@ -225,7 +223,12 @@
                         for copy in beside_far:
                             copy.start()
 
-    lax.fori_loop(0, window - 1, start_answer, 0)
+        @pl.when((core == 1) & (x == 0))
+        def _():
+            for copy in far_direct:
+                copy.start()
+
+    lax.fori_loop(ahead, window - 1, start_answer, 0)
 
     to_users = pltpu.make_async_copy(users, user_scalars, scalar_sem)
     to_users.start()
@@ -358,6 +361,11 @@
             for copy in beside_far:
                 copy.wait_send()
 
+        @pl.when((core == 1) & (x == 0))
+        def _():
+            for copy in far_direct:
+                copy.wait_send()
+
     def end_ask(owner, carry):
         ask(owner).wait_send()
         return carry
@@ -371,40 +379,98 @@
     lax.fori_loop(me + 1, window, end_answer, 0)
 
 
-def merge_kernel(blocks, slots, partial, stats, *rest):
-    slot_count = blocks * PICKED_BLOCKS
-    slot_partials, slot_stats, out = rest[:slot_count], rest[slot_count:-1], rest[-1]
-    head = pl.program_id(0)
-    row = lax.broadcasted_iota(jnp.int32, (BLOCK_TOKENS, BLOCK_TOKENS), 0)
-    column = lax.broadcasted_iota(jnp.int32, (BLOCK_TOKENS, BLOCK_TOKENS), 1)
-    identity = jnp.where(row == column, 1.0, 0.0).astype(jnp.bfloat16)
-    for i in range(blocks):
-        alive = slots[0, (i * KEY_VALUE_HEADS + head) * PICKED_BLOCKS] >= 0
-        rows = slice(i * BLOCK_TOKENS, (i + 1) * BLOCK_TOKENS)
-        pair = range(i * PICKED_BLOCKS, (i + 1) * PICKED_BLOCKS)
-
-        def give(part, result):
-            for n in range(CHUNK):
-                at = (part * CHUNK + n) * HEAD_SIZE
-                turned = dot_nt(identity, result[:, n * BLOCK_TOKENS : (n + 1) * BLOCK_TOKENS].astype(jnp.bfloat16))
-                out[rows, at : at + HEAD_SIZE] = turned.astype(jnp.bfloat16)
-
-        @pl.when(alive)
+def merge_kernel(
+    blocks, slots, partial, stats, slot_partial, slot_stats, out,
+    partial_held, stats_held, slot_partial_held, slot_stats_held, out_held, load_sem, slot_sem, stats_sem, store_sem,
+):
+    ahead = 3
+    per_head = out_held.shape[2]
+
+    def first_pick(h, i):
+        return (i * KEY_VALUE_HEADS + h) * PICKED_BLOCKS
+
+    def load(h):
+        return pltpu.make_async_copy(partial.at[h], partial_held.at[h], load_sem.at[h])
+
+    def load_slot(at):
+        slot = jnp.maximum(slots[0, at], 0)
+        return pltpu.make_async_copy(slot_partial.at[slot], slot_partial_held.at[at], slot_sem.at[at])
+
+    def store(h):
+        columns = pl.ds(pl.multiple_of(h * per_head, per_head), per_head)
+        return pltpu.make_async_copy(out_held.at[h], out.at[:, columns], store_sem.at[h])
+
+    def start(h, carry):
+        load(h).start()
+        for i in range(blocks):
+            at = first_pick(h, i)
+
+            @pl.when(slots[0, at] >= 0)
+            def _():
+                for p in range(PICKED_BLOCKS):
+                    load_slot(at + p).start()
+
+        return carry
+
+    all_stats = [
+        pltpu.make_async_copy(stats, stats_held, stats_sem.at[0]),
+        pltpu.make_async_copy(slot_stats, slot_stats_held, stats_sem.at[1]),
+    ]
+    for copy in all_stats:
+        copy.start()
+    lax.fori_loop(0, ahead, start, 0)
+    for copy in all_stats:
+        copy.wait()
+
+    def one_head(h, carry):
+        @pl.when(h + ahead < KEY_VALUE_HEADS)
         def _():
-            for part in range(GROUP // CHUNK):
-                here = slice(part * CHUNK * BLOCK_TOKENS, (part + 1) * CHUNK * BLOCK_TOKENS)
-                logs = [stats[0, i, :, here]] + [slot_stats[p][0, :, here] for p in pair]
-                terms = [partial[0, i, :, here]] + [slot_partials[p][0, :, here] for p in pair]
-                top = functools.reduce(jnp.maximum, logs)
-                weights = [jnp.exp2(log - top) for log in logs]
-                inverse = 1.0 / sum(weights)
-                give(part, sum(t.astype(jnp.float32) * (w * inverse) for t, w in zip(terms, weights)))
-
-        @pl.when(jnp.logical_not(alive))
-        def _():
-            for part in range(GROUP // CHUNK):
-                here = slice(part * CHUNK * BLOCK_TOKENS, (part + 1) * CHUNK * BLOCK_TOKENS)
-                give(part, partial[0, i, :, here].astype(jnp.float32))
+            start(h + ahead, 0)
+
+        load(h).wait()
+        for i in range(blocks):
+            at = first_pick(h, i)
+            alive = slots[0, at] >= 0
+            rows = slice(i * BLOCK_TOKENS, (i + 1) * BLOCK_TOKENS)
+
+            def give(part, result):
+                for n in range(CHUNK):
+                    place = (part * CHUNK + n) * HEAD_SIZE
+                    turned = result[:, n * BLOCK_TOKENS : (n + 1) * BLOCK_TOKENS].T
+                    out_held[h, rows, place : place + HEAD_SIZE] = turned.astype(jnp.bfloat16)
+
+            @pl.when(alive)
+            def _():
+                for p in range(PICKED_BLOCKS):
+                    load_slot(at + p).wait()
+                for part in range(GROUP // CHUNK):
+                    here = slice(part * CHUNK * BLOCK_TOKENS, (part + 1) * CHUNK * BLOCK_TOKENS)
+                    logs = [stats_held[h, i, :, here]]
+                    terms = [partial_held[h, i, :, here]]
+                    for p in range(PICKED_BLOCKS):
+                        logs.append(slot_stats_held[slots[0, at + p], :, here])
+                        terms.append(slot_partial_held[at + p, :, here])
+                    top = functools.reduce(jnp.maximum, logs)
+                    weights = [jnp.exp2(log - top) for log in logs]
+                    inverse = 1.0 / sum(weights)
+                    give(part, sum(t.astype(jnp.float32) * (w * inverse) for t, w in zip(terms, weights)))
+
+            @pl.when(jnp.logical_not(alive))
+            def _():
+                for part in range(GROUP // CHUNK):
+                    here = slice(part * CHUNK * BLOCK_TOKENS, (part + 1) * CHUNK * BLOCK_TOKENS)
+                    give(part, partial_held[h, i, :, here].astype(jnp.float32))
+
+        store(h).start()
+        return carry
+
+    lax.fori_loop(0, KEY_VALUE_HEADS, one_head, 0)
+
+    def end_store(h, carry):
+        store(h).wait()
+        return carry
+
+    lax.fori_loop(0, KEY_VALUE_HEADS, end_store, 0)
 
 
 def shards(queries, keys, values, positions, picks):
@@ -489,34 +555,25 @@
         name="exchange_and_band",
     )(queries, keys, values, cosine, sine, picks.reshape(1, count))
 
-    def slot_specs(dims):
-        def spec(at):
-            def place(h, slot):
-                i, p = at // PICKED_BLOCKS, at % PICKED_BLOCKS
-                return (jnp.maximum(slot[0, (i * KEY_VALUE_HEADS + h) * PICKED_BLOCKS + p], 0), 0, 0)
-
-            return pl.BlockSpec((1,) + dims, place)
-
-        return [spec(at) for at in range(blocks * PICKED_BLOCKS)]
-
-    def head_spec(dims):
-        return pl.BlockSpec((1,) + dims[1:], lambda h, *_: (h, 0, 0, 0))
-
-    copies = blocks * PICKED_BLOCKS
     return pl.pallas_call(
         functools.partial(merge_kernel, blocks),
-        grid_spec=pltpu.PrefetchScalarGridSpec(
-            num_scalar_prefetch=1,
-            grid=(KEY_VALUE_HEADS,),
-            in_specs=[head_spec(partial_dims), head_spec(stats_dims)]
-            + slot_specs((HEAD_SIZE, stacked))
-            + slot_specs((1, stacked)),
-            out_specs=pl.BlockSpec((tokens, per_head), lambda h, *_: (0, h)),
-        ),
+        in_specs=[pl.BlockSpec(memory_space=pltpu.SMEM)] + [there] * 4,
+        out_specs=there,
         out_shape=jax.ShapeDtypeStruct(queries.shape, jnp.bfloat16),
+        scratch_shapes=[
+            pltpu.VMEM(partial_dims, jnp.bfloat16),
+            pltpu.VMEM(stats_dims, jnp.float32),
+            pltpu.VMEM((count, HEAD_SIZE, stacked), jnp.bfloat16),
+            pltpu.VMEM((slot_count, 1, stacked), jnp.float32),
+            pltpu.VMEM(by_head, jnp.bfloat16),
+            pltpu.SemaphoreType.DMA((KEY_VALUE_HEADS,)),
+            pltpu.SemaphoreType.DMA((count,)),
+            pltpu.SemaphoreType.DMA((2,)),
+            pltpu.SemaphoreType.DMA((KEY_VALUE_HEADS,)),
+        ],
         compiler_params=pltpu.CompilerParams(vmem_limit_bytes=limit),
         name="merge",
-    )(slots, partial, stats, *[slot_partial] * copies, *[slot_stats] * copies)
+    )(slots, partial, stats, slot_partial, slot_stats)
 
 
 def solution(mesh):

time: 91.3 us -> 92.6 us (1.014)
  the two profiles are of different devices: /device:TPU:27 before, /device:TPU:17 now
where the time goes in v5:
time: 92.6 us; the launch traced here: 92.4 us
  Pallas kernels  88.9 us (96%)
  other arithmetic  2.07 us (2%)
  local copies, waits for them, and re-layouts  1.39 us (2%)
    pallas_call x1, Pallas kernels, shards(): pl.pallas_call(functools.partial(exchange_kernel, blocks, window, cap, wi...  81.7 us
    pallas_call x1, Pallas kernels, shards(): pl.pallas_call(functools.partial(merge_kernel, blocks), in_specs=[pl.Bloc...  7.23 us

profile of v5, /device:TPU:17, one launch (start us, length us, event | category | flops | bytes accessed | tf_op | source)
XLA Modules:
  0.0 92.4 jit_solution(17148235818768621931)
XLA Ops:
  0.0 0.7 convert_element_type.3
  0.7 0.8 copy.7
  1.5 0.6 reshape.11.pick_row
  2.1 0.5 fusion
  2.6 0.8 pad_maximum_fusion
  3.5 81.7 %exchange_and_band.1 = (bf16[8,2,128,1024]{3,2,1,0:T(8,128)(2,1)}, f32[8,2,1,1024]{3,2,1,0:T(1,128)}, bf16[32,128,1024]{2,1,0:T(8,128)(2,1)}, f32[32,1,1024]{2,1,0:T(1,128)}, s32[1,32]{1,0:T(1,128)}) custom-call(bf16[256,8192]{1,0:T(8,128)(2,1)} %queries.1, bf16[256,1024]{1,0:T(8,128)(2,1)} %keys.1, bf16[256,1024]{1,0:T(8,128)(2,1)} %values.1, ...), custom_call_target="tpu_custom_call" | custom-call | flops 4294967296 | bytes 12582912 | tf_op jit(solution)/shard_map/exchange_and_band/pallas_call | solution.py:502
  85.1 7.2 %merge.1 = bf16[256,8192]{1,0:T(8,128)(2,1)} custom-call(s32[1,32]{1,0:T(1,128)} %get-tuple-element.10.slots, bf16[8,2,128,1024]{3,2,1,0:T(8,128)(2,1)} %get-tuple-element.11.partial, f32[8,2,1,1024]{3,2,1,0:T(1,128)} %get-tuple-element.12.stats, bf16[32,128,1024]{2,1,0:T(8,128)(2,1)} %get-tuple-element.13.slot_partial, ...), custom_call_target="tpu_custom_call" | custom-call | tf_op jit(solution)/shard_map/merge/pallas_call | solution.py:558
  (1 shorter events, 0.0 us)

commit v6 on v5

--- a/solution.py
+++ b/solution.py
@@ -208,7 +208,7 @@
 
         return carry
 
-    ahead = 2
+    ahead = 1
     lax.fori_loop(0, ahead, start_answer, 0)
 
     if relays:
@@ -234,16 +234,6 @@
     to_users.start()
     to_users.wait()
 
-    @pl.when(me >= 1)
-    def _():
-        for copy in near_direct:
-            copy.wait_recv()
-
-    @pl.when(me >= 2)
-    def _():
-        for copy in far_direct:
-            copy.wait_recv()
-
     width = LOCAL_BAND_SIZE * BLOCK_TOKENS
     factor = HEAD_SIZE**-0.5 * log2_e
     key = lax.broadcasted_iota(jnp.int32, (width, BLOCK_TOKENS), 0)
@@ -255,39 +245,17 @@
             pltpu.make_async_copy(stats_held.at[h], stats.at[h], store_sem.at[1, h]),
         ]
 
-    def one_head(h, carry):
+    def rotate_head(h, carry):
         load(h).wait()
-        band = [far[h]] + [near[i * KEY_VALUE_HEADS + h] for i in range(blocks)]
-        band = band + [kv[i * KEY_VALUE_HEADS + h] for i in range(blocks)]
-        k_all = jnp.concatenate([b[0] for b in band], 0)
-        v_all = with_ones(jnp.concatenate([b[1] for b in band], 1))
         for i in range(blocks):
-            start = (me * blocks + i - (LOCAL_BAND_SIZE - 1)) * BLOCK_TOKENS
-            good = (key <= query + (LOCAL_BAND_SIZE - 1) * BLOCK_TOKENS) & (key + start >= 0)
-            bias = jnp.concatenate([jnp.where(good, 0.0, masked_score)] * CHUNK, 1)
             rows = slice(i * BLOCK_TOKENS, (i + 1) * BLOCK_TOKENS)
-            k = k_all[i * BLOCK_TOKENS : i * BLOCK_TOKENS + width]
-            v = v_all[:, i * BLOCK_TOKENS : i * BLOCK_TOKENS + width]
             q_cosine, q_sine = cosine[rows] * factor, sine[rows] * factor
-            for part in range(GROUP // CHUNK):
-                here = slice(part * CHUNK * BLOCK_TOKENS, (part + 1) * CHUNK * BLOCK_TOKENS)
-                heads = range(part * CHUNK, (part + 1) * CHUNK)
-                q = jnp.concatenate(
-                    [rotate(q_held[h, rows, n * HEAD_SIZE : (n + 1) * HEAD_SIZE], q_cosine, q_sine) for n in heads], 0
-                ).astype(jnp.bfloat16)
-                rotated[i * KEY_VALUE_HEADS + h, here] = q
-                score = dot_nt(k, q) + bias
-                top = jnp.max(score, 0, keepdims=True)
-                weight = jnp.exp2(score - top).astype(jnp.bfloat16)
-                summed = jnp.dot(v, weight, preferred_element_type=jnp.float32)
-                total = summed[HEAD_SIZE : HEAD_SIZE + 1]
-                partial_held[h, i, :, here] = (summed[:HEAD_SIZE] * (1.0 / total)).astype(jnp.bfloat16)
-                stats_held[h, i, :, here] = top + jnp.log2(total)
-        for copy in store(h):
-            copy.start()
-        return carry
-
-    lax.fori_loop(0, KEY_VALUE_HEADS, one_head, 0)
+            for n in range(GROUP):
+                q = rotate(q_held[h, rows, n * HEAD_SIZE : (n + 1) * HEAD_SIZE], q_cosine, q_sine)
+                rotated[i * KEY_VALUE_HEADS + h, n * BLOCK_TOKENS : (n + 1) * BLOCK_TOKENS] = q.astype(jnp.bfloat16)
+        return carry
+
+    lax.fori_loop(0, KEY_VALUE_HEADS, rotate_head, 0)
 
     def store_slots(source, side):
         place = pl.ds(source * cap, cap)
@@ -325,7 +293,47 @@
 
         return done + jnp.where(source < me, 1, 0)
 
-    lax.fori_loop(0, window - 1, one_source, jnp.int32(0))
+    early = min(3, window - 1)
+    done = lax.fori_loop(0, early, one_source, jnp.int32(0))
+
+    @pl.when(me >= 1)
+    def _():
+        for copy in near_direct:
+            copy.wait_recv()
+
+    @pl.when(me >= 2)
+    def _():
+        for copy in far_direct:
+            copy.wait_recv()
+
+    def one_head(h, carry):
+        band = [far[h]] + [near[i * KEY_VALUE_HEADS + h] for i in range(blocks)]
+        band = band + [kv[i * KEY_VALUE_HEADS + h] for i in range(blocks)]
+        k_all = jnp.concatenate([b[0] for b in band], 0)
+        v_all = with_ones(jnp.concatenate([b[1] for b in band], 1))
+        for i in range(blocks):
+            start = (me * blocks + i - (LOCAL_BAND_SIZE - 1)) * BLOCK_TOKENS
+            good = (key <= query + (LOCAL_BAND_SIZE - 1) * BLOCK_TOKENS) & (key + start >= 0)
+            bias = jnp.concatenate([jnp.where(good, 0.0, masked_score)] * CHUNK, 1)
+            k = k_all[i * BLOCK_TOKENS : i * BLOCK_TOKENS + width]
+            v = v_all[:, i * BLOCK_TOKENS : i * BLOCK_TOKENS + width]
+            for part in range(GROUP // CHUNK):
+                here = slice(part * CHUNK * BLOCK_TOKENS, (part + 1) * CHUNK * BLOCK_TOKENS)
+                q = rotated[i * KEY_VALUE_HEADS + h, here]
+                score = dot_nt(k, q) + bias
+                top = jnp.max(score, 0, keepdims=True)
+                weight = jnp.exp2(score - top).astype(jnp.bfloat16)
+                summed = jnp.dot(v, weight, preferred_element_type=jnp.float32)
+                total = summed[HEAD_SIZE : HEAD_SIZE + 1]
+                partial_held[h, i, :, here] = (summed[:HEAD_SIZE] * (1.0 / total)).astype(jnp.bfloat16)
+                stats_held[h, i, :, here] = top + jnp.log2(total)
+        for copy in store(h):
+            copy.start()
+        return carry
+
+    lax.fori_loop(0, KEY_VALUE_HEADS, one_head, 0)
+
+    lax.fori_loop(early, window - 1, one_source, done)
 
     def end_slots(source, carry):
         for copy in store_slots(source, source % 2):

time: 92.6 us -> 89 us (0.961)
  Pallas kernels: 88.9 us -> 85.3 us
    pallas_call x1, Pallas kernels: 81.7 us -> 78.1 us  [shards(): pl.pallas_call(functools.partial(exchange_kernel, blocks, window, cap, wi...]
where the time goes in v6:
time: 89 us; the launch traced here: 88.8 us
  Pallas kernels  85.3 us (96%)
  other arithmetic  2.07 us (2%)
  local copies, waits for them, and re-layouts  1.39 us (2%)
    pallas_call x1, Pallas kernels, shards(): pl.pallas_call(functools.partial(exchange_kernel, blocks, window, cap, wi...  78.1 us
    pallas_call x1, Pallas kernels, shards(): pl.pallas_call(functools.partial(merge_kernel, blocks), in_specs=[pl.Bloc...  7.23 us

profile of v6, /device:TPU:17, one launch (start us, length us, event | category | flops | bytes accessed | tf_op | source)
XLA Modules:
  0.0 88.8 jit_solution(7395549868467281786)
XLA Ops:
  0.0 0.7 convert_element_type.3
  0.7 0.8 copy.7
  1.5 0.6 reshape.11.pick_row
  2.1 0.5 fusion
  2.6 0.8 pad_maximum_fusion
  3.5 78.1 %exchange_and_band.1 = (bf16[8,2,128,1024]{3,2,1,0:T(8,128)(2,1)}, f32[8,2,1,1024]{3,2,1,0:T(1,128)}, bf16[32,128,1024]{2,1,0:T(8,128)(2,1)}, f32[32,1,1024]{2,1,0:T(1,128)}, s32[1,32]{1,0:T(1,128)}) custom-call(bf16[256,8192]{1,0:T(8,128)(2,1)} %queries.1, bf16[256,1024]{1,0:T(8,128)(2,1)} %keys.1, bf16[256,1024]{1,0:T(8,128)(2,1)} %values.1, ...), custom_call_target="tpu_custom_call" | custom-call | flops 4294967296 | bytes 12582912 | tf_op jit(solution)/shard_map/exchange_and_band/pallas_call | solution.py:510
  81.5 7.2 %merge.1 = bf16[256,8192]{1,0:T(8,128)(2,1)} custom-call(s32[1,32]{1,0:T(1,128)} %get-tuple-element.10.slots, bf16[8,2,128,1024]{3,2,1,0:T(8,128)(2,1)} %get-tuple-element.11.partial, f32[8,2,1,1024]{3,2,1,0:T(1,128)} %get-tuple-element.12.stats, bf16[32,128,1024]{2,1,0:T(8,128)(2,1)} %get-tuple-element.13.slot_partial, ...), custom_call_target="tpu_custom_call" | custom-call | tf_op jit(solution)/shard_map/merge/pallas_call | solution.py:566
  (1 shorter events, 0.0 us)
